TPU v7x, 128 devices: a whole 4x4x4 slice. The times are simulated.
128 devices in a mesh: dp: 16 (over z, y), row: 2 (over x_hi), col: 4 (over x_lo, core).
Axes of the slice: x: 4 (x_hi: 2, x_lo: 2; x = x_hi * 2 + x_lo), y: 4, z: 4, core: 2. Of those that a mesh axis runs over, the one named last changes fastest.
Arguments:
- tokens: bfloat16 [16384, 1152], P(('dp', 'row', 'col')), may hold values from -6 to 6
- cotangent: bfloat16 [16384, 1152], P(('dp', 'row', 'col')), may hold values from -6 to 6
- branch: int32 [16, 2], P('dp'), may hold values from 256 to 512, as said below
- w_query: float32 [2, 576, 4, 256], P('row', 'dp', 'col'), may hold values from -0.1875 to 0.1875
- w_keyval: float32 [2, 2, 576, 256], P(None, 'row', 'dp'), may hold values from -0.1875 to 0.1875
- w_out: float32 [4, 256, 2, 576], P('col', None, 'row', 'dp'), may hold values from -0.1875 to 0.1875
- w_gate_up: float32 [2, 4, 16, 124416], P('row', 'col', 'dp'), may hold values from -0.1875 to 0.1875
- w_down: float32 [2, 4, 16, 62208], P('row', 'col', 'dp'), may hold values from -0.078125 to 0.078125
- mom_query: float32 [2, 576, 4, 256], P('row', 'dp', 'col'), may hold values from -160 to 160
- mom_keyval: float32 [2, 2, 576, 256], P(None, 'row', 'dp'), may hold values from -160 to 160
- mom_out: float32 [4, 256, 2, 576], P('col', None, 'row', 'dp'), may hold values from -160 to 160
- mom_gate_up: float32 [2, 4, 16, 124416], P('row', 'col', 'dp'), may hold values from -320 to 320
- mom_down: float32 [2, 4, 16, 62208], P('row', 'col', 'dp'), may hold values from -384 to 384
- norm_gains: float32 [4, 1152], replicated
- qk_gains: float32 [2, 256], replicated, may hold values from 0.25 to 1.75
- mom_norm: float32 [4, 1152], replicated, may hold values from -768 to 768
- mom_qk: float32 [2, 256], replicated, may hold values from -224 to 224
Outputs:
- layer_out: bfloat16 [16384, 1152], P(('dp', 'row', 'col'))
- input_grad: float32 [16384, 1152], P(('dp', 'row', 'col'))
- new_mom_query: float32 [2, 576, 4, 256], P('row', 'dp', 'col')
- new_query: float32 [2, 576, 4, 256], P('row', 'dp', 'col')
- low_query: bfloat16 [2, 576, 4, 256], P('row', 'dp', 'col')
- new_mom_keyval: float32 [2, 2, 576, 256], P(None, 'row', 'dp')
- new_keyval: float32 [2, 2, 576, 256], P(None, 'row', 'dp')
- low_keyval: bfloat16 [2, 2, 576, 256], P(None, 'row', 'dp')
- new_mom_out: float32 [4, 256, 2, 576], P('col', None, 'row', 'dp')
- new_out: float32 [4, 256, 2, 576], P('col', None, 'row', 'dp')
- low_out: bfloat16 [4, 256, 2, 576], P('col', None, 'row', 'dp')
- new_mom_gate_up: float32 [2, 4, 16, 124416], P('row', 'col', 'dp')
- new_gate_up: float32 [2, 4, 16, 124416], P('row', 'col', 'dp')
- low_gate_up: bfloat16 [2, 4, 16, 124416], P('row', 'col', 'dp')
- new_mom_down: float32 [2, 4, 16, 62208], P('row', 'col', 'dp')
- new_down: float32 [2, 4, 16, 62208], P('row', 'col', 'dp')
- low_down: bfloat16 [2, 4, 16, 62208], P('row', 'col', 'dp')
- new_mom_norm: float32 [4, 1152], replicated
- new_norm_gains: float32 [4, 1152], replicated
- new_mom_qk: float32 [2, 256], replicated
- new_qk_gains: float32 [2, 256], replicated
Inputs may be any that keep to these rules, and one draw needn't show every extreme that they name: Continuation c of a replica follows the first branch[replica, c] prompt tokens and starts at that position; in every replica one continuation follows the whole prompt, 512 tokens.
All inputs are finite; a program needn't handle non-finite values.
Results may differ from a plain program's by a relative error of at most 0.0169.
Values may be sent and summed in bfloat16 or wider, within the bound.
No kernel may reach another device: no remote copies, remote signals or barrier semaphores. Data moves between devices by JAX's collectives and lax.ppermute only.
A program may use at most 192 MiB of HBM per device.

v0:
```python
import functools
import math

import jax
import jax.numpy as jnp
from jax import lax
from jax.experimental import pallas as pl
from jax.experimental.pallas import tpu as pltpu
from jax.sharding import PartitionSpec as P

CONT_LEN = 256
WINDOW = 512
NS_STEPS = 5
NORM_EPS = 1e-06
MUON_EPS = 1e-07
COEF_A = 3.4445
COEF_B = -4.775
COEF_C = 2.0315
MUON_RATE = 0.5
MUON_DECAY = 0.5
WEIGHT_DECAY = 0.01
GAIN_RATE = 0.003
GAIN_MOMENTUM = 0.5
ROPE_BASE = 10000.0
HIGH = lax.Precision.HIGHEST
BF = jnp.bfloat16
F32 = jnp.float32
RING = ("row", "col")
MASKED = -1e30
MIB = 2**20
PAD = 64
GELU_C = math.sqrt(2.0 / math.pi)

NN = (((1,), (0,)), ((), ()))
NT = (((1,), (1,)), ((), ()))
TN = (((0,), (0,)), ((), ()))


def mm(left, right, dims=NN, precision=None):
    return lax.dot_general(left, right, dims, precision=precision, preferred_element_type=F32)


def flip(block, bits):
    return lax.ppermute(block, RING, [(i, i ^ bits) for i in range(8)])


def gather4(block):
    near = [block, flip(block, 2)]
    return near + [flip(part, 1) for part in near]


def gather8(block):
    near = [flip(block, 4), flip(block, 6)]
    return gather4(block) + near + [flip(part, 1) for part in near]


def scatter8(parts):
    def paired(near, far):
        return near.astype(F32) + flip(far, 1).astype(F32)

    across, last = paired(parts[4], parts[6]), paired(parts[5], parts[7])
    beside, total = paired(parts[1], parts[3]), paired(parts[0], parts[2])
    for value, bits in ((across, 4), (last, 6), (beside, 2)):
        total = total + flip(value.astype(BF), bits).astype(F32)
    return total


def scatter4(parts):
    beside = parts[1].astype(F32) + flip(parts[3], 1).astype(F32)
    total = parts[0].astype(F32) + flip(parts[2], 1).astype(F32)
    return total + flip(beside.astype(BF), 2).astype(F32)


def after(value, *others):
    return lax.optimization_barrier((value,) + others)[0]


def swap_all(blocks):
    return lax.all_to_all(blocks, "dp", 0, 0, tiled=True)


def inv_rms(vector):
    return lax.rsqrt(jnp.mean(vector * vector, axis=-1, keepdims=True) + NORM_EPS)


def norm_back(vector, gain, grad):
    scale = inv_rms(vector)
    gz = grad * gain
    du = scale * gz - vector * (scale * scale * scale) * jnp.mean(
        gz * vector, axis=-1, keepdims=True
    )
    return du, jnp.sum(grad * vector * scale, axis=0, keepdims=True)


def rotate(vector, cosine, sine):
    half = vector.shape[-1] // 2
    first, second = vector[:, :half], vector[:, half:]
    return jnp.concatenate([first * cosine - second * sine, second * cosine + first * sine], axis=1)


def rotate_back(vector, cosine, sine):
    half = vector.shape[-1] // 2
    first, second = vector[:, :half], vector[:, half:]
    return jnp.concatenate([first * cosine + second * sine, second * cosine - first * sine], axis=1)


def own_rows(values):
    return values[: values.shape[0] // 2]


def join(*parts):
    return jnp.concatenate([part[...] for part in parts], axis=0)


def attn_fwd_kernel(*refs):
    xs, (w_all, mask, cos, sin, gains), bs = refs[:8], refs[8:13], refs[13:17]
    w, qraw_o, kraw_o, q_o, k_o, v_o, att_o, lse_o = refs[17:]
    hd = q_o.shape[1]
    half = w.shape[0] // 2
    slab = w_all.shape[1] // 2
    slabs = [w_all[d].astype(F32) for d in range(w_all.shape[0])]
    for side in (0, 1):
        rows = [both[side * slab : (side + 1) * slab] for both in slabs]
        w[side * half : (side + 1) * half, :] = jnp.concatenate(rows, axis=0).astype(BF)
    x = join(*xs)
    qraw = mm(own_rows(x), w[:, :hd])
    kv = mm(x, w[:, hd : 3 * hd])
    kraw = kv[:, :hd]
    cosine, sine = cos[...], sin[...]
    q = rotate(qraw * inv_rms(qraw) * gains[0:1, :], own_rows(cosine), own_rows(sine)).astype(BF)
    k = rotate(kraw * inv_rms(kraw) * gains[1:2, :], cosine, sine).astype(BF)
    v = kv[:, hd:].astype(BF)
    scores = mm(q, k, NT) * (hd**-0.5) + mask[...].astype(F32)
    largest = jnp.max(scores, axis=1, keepdims=True)
    weights = jnp.exp(scores - largest)
    total = jnp.sum(weights, axis=1, keepdims=True)
    att = mm((weights / total).astype(BF), v).astype(BF)
    branch = mm(att, w[:, 3 * hd :], NT).astype(BF)
    rows = bs[0].shape[0]
    for i, part in enumerate(bs):
        part[...] = branch[i * rows : (i + 1) * rows]
    qraw_o[...] = qraw
    kraw_o[...] = kraw
    q_o[...] = q
    k_o[...] = k
    v_o[...] = v
    att_o[...] = att
    lse_o[...] = jnp.broadcast_to(largest + jnp.log(total), lse_o.shape)


def attn_bwd_kernel(*refs):
    das, xs, refs = refs[:4], refs[4:12], refs[12:]
    w, mask, cos, sin, gains, qraw, kraw, q, k, v, att, lse = refs[:12]
    ns, (dw, dgains) = refs[12:20], refs[20:]
    hd = q.shape[1]
    half = q.shape[0]
    scale = hd**-0.5
    da = join(*das)
    datt = mm(da, w[:, 3 * hd :]).astype(BF)
    scores = mm(q[...], k[...], NT) * scale + mask[...].astype(F32)
    weights = jnp.exp(scores - lse[:, 0:1])
    dv = mm(weights.astype(BF), datt, TN).astype(BF)
    dp = mm(datt, v[...], NT)
    inner = jnp.sum(weights * dp, axis=1, keepdims=True)
    ds = (weights * (dp - inner)).astype(BF)
    dq = mm(ds, k[...]) * scale
    dk = mm(ds, q[...], TN) * scale
    cosine, sine = cos[...], sin[...]
    dqraw, dgq = norm_back(
        qraw[...], gains[0:1, :], rotate_back(dq, own_rows(cosine), own_rows(sine))
    )
    dkraw, dgk = norm_back(kraw[...], gains[1:2, :], rotate_back(dk, cosine, sine))
    dqraw, dkraw = dqraw.astype(BF), dkraw.astype(BF)
    dgains[0:1, :] = dgq
    dgains[1:2, :] = dgk
    x = join(*xs)
    width = x.shape[1]
    parts = (
        (mm(own_rows(x), dqraw, TN), 0),
        (mm(x, dkraw, TN), 1),
        (mm(x, dv, TN), 2),
        (mm(da, att[...], TN), 3),
    )
    slab = dw.shape[1] // 2
    for part, place in parts:
        for d in range(dw.shape[0]):
            both = [part[at : at + slab] for at in (d * slab, width // 2 + d * slab)]
            dw[d, :, place * hd : (place + 1) * hd] = jnp.concatenate(both, axis=0).astype(BF)
    back = mm(dkraw, w[:, hd : 2 * hd], NT) + mm(dv, w[:, 2 * hd : 3 * hd], NT)
    qback = mm(dqraw, w[:, :hd], NT)
    rows = ns[0].shape[0]
    for i, part in enumerate(ns):
        at = slice(i * rows, (i + 1) * rows)
        part[...] = (back[at] + qback[at] if i < 4 else back[at]).astype(BF)


def gelu_parts(gate):
    cube = GELU_C * 0.044715
    square = gate * gate
    h = 0.5 * jnp.tanh(gate * (cube * square + GELU_C)) + 0.5
    value = gate * h
    slope = h + value * (1.0 - h) * (6.0 * cube * square + 2.0 * GELU_C)
    return value, slope


def ffn_fwd_kernel(*refs):
    xs, w, (slope_o, value_o, hidden_o), parts = refs[:8], refs[8], refs[9:12], refs[12:20]
    x, units, down = refs[20:]
    step = pl.program_id(0)
    slabs, _, rows, width = w.shape
    count = slabs * rows

    @pl.when(step == 0)
    def _():
        gather_rows(x, xs)

    gate = mm(x[...], w[:, 0].reshape(count, width), NT)
    up = mm(x[...], w[:, 1].reshape(count, width), NT)
    value, slope = gelu_parts(gate)
    hidden = (value * up).astype(BF)
    slope_o[...] = (slope * up).astype(BF)
    value_o[...] = value.astype(BF)
    hidden_o[...] = hidden
    units[step] = hidden
    down[pl.ds(pl.multiple_of(step * count, count), count), :] = w[:, 2].reshape(count, width)

    @pl.when(step == pl.num_programs(0) - 1)
    def _():
        whole = jnp.concatenate([units[i] for i in range(units.shape[0])], axis=1)
        total = mm(whole, down[...]).astype(BF)
        height = parts[0].shape[0]
        for i, part in enumerate(parts):
            part[...] = total[i * height : (i + 1) * height]


def gather_rows(whole, parts):
    height = parts[0].shape[0]
    for i, part in enumerate(parts):
        whole[i * height : (i + 1) * height, :] = part[...]


def accumulate(step, acc, term, *parts):
    last = pl.num_programs(0) - 1

    @pl.when(step == 0)
    def _():
        acc[...] = term

    @pl.when((step > 0) & (step < last))
    def _():
        acc[...] += term

    @pl.when(step == last)
    def _():
        total = (acc[...] + term).astype(BF)
        rows = parts[0].shape[0]
        for i, part in enumerate(parts):
            part[...] = total[i * rows : (i + 1) * rows]


def ffn_units_kernel(*refs):
    xs, ds, refs = refs[:8], refs[8:16], refs[16:]
    w, slope_i, value_i, hidden_i, dgate_o, dup_o, dw, x, d = refs
    slabs, _, rows, width = dw.shape

    @pl.when(pl.program_id(0) == 0)
    def _():
        gather_rows(x, xs)
        gather_rows(d, ds)

    dhid = mm(d[...], w[...].reshape(slabs * rows, width), NT)
    dgate = (dhid * slope_i[...].astype(F32)).astype(BF)
    dup = (dhid * value_i[...].astype(F32)).astype(BF)
    dgate_o[...] = dgate
    dup_o[...] = dup
    for i, (left, right) in enumerate(((dgate, x), (dup, x), (hidden_i[...], d))):
        dw[:, i] = mm(left, right[...], TN).astype(BF).reshape(slabs, rows, width)


def ffn_tokens_kernel(dgate, dup, w, *refs):
    parts, acc = refs[:8], refs[8]
    slabs, _, rows, width = w.shape
    term = mm(dgate[...], w[:, 0].reshape(slabs * rows, width)) + mm(
        dup[...], w[:, 1].reshape(slabs * rows, width)
    )
    accumulate(pl.program_id(0), acc, term, *parts)


def split(values, count):
    pieces = []
    for _ in range(count):
        pieces.append(values.astype(BF))
        values = values - pieces[-1].astype(F32)
    return pieces


def stacks(values):
    a, b = split(values, 2)
    return jnp.concatenate([a, a, b], axis=0), jnp.concatenate([a, b, a], axis=0)


def sym_parts(left, right, n):
    return [mm(left[:, at:], right[:, at : at + 256], TN) for at in range(0, n, 256)]


def sym_full(parts):
    columns = []
    for j, part in enumerate(parts):
        above = [parts[i][(j - i) * 256 : (j - i) * 256 + part.shape[1]].T for i in range(j)]
        columns.append(jnp.concatenate(above + [part], axis=0) if above else part)
    return jnp.concatenate(columns, axis=1) if len(columns) > 1 else columns[0]


def sym_mm(left, right, n):
    return sym_full(sym_parts(left, right, n))


def muon_chains(grams, currents):
    n = grams[0].shape[0]
    diag = lax.broadcasted_iota(jnp.int32, (n, n), 0) == lax.broadcasted_iota(jnp.int32, (n, n), 1)
    a, x = [], []
    for gram, current in zip(grams, currents):
        trace = jnp.sum(
            jnp.sum(jnp.where(diag, gram, 0.0), axis=1, keepdims=True), axis=0, keepdims=True
        )
        factor = 1.0 / (jnp.sqrt(trace) + MUON_EPS)
        a.append(gram * (factor * factor))
        x.append(current * factor)
    for step in range(NS_STEPS):
        sa = [stacks(m) for m in a]
        square = [sym_mm(l, r, n) for l, r in sa]
        poly = [COEF_B * m + COEF_C * q + jnp.where(diag, COEF_A, 0.0) for m, q in zip(a, square)]
        sp = [stacks(p) for p in poly]
        if step < NS_STEPS - 1:
            half = [stacks(sym_mm(l, sp[i][1], n)) for i, (l, _) in enumerate(sa)]
            a = [sym_mm(l, sp[i][1], n) for i, (l, _) in enumerate(half)]
        x = [mm(sp[i][0], stacks(m)[1], TN) for i, m in enumerate(x)]
    return x


def pack_rows(n):
    return sum(2 * (n - at) if n - at >= 256 else n - at for at in range(0, n, 256))


def ff_gram_kernel(flag, mine, theirs, mom_gu, mom_d, gu_o, d_o, gu_c, d_c, packed):
    first = flag[0] == 0
    n = mom_gu.shape[0]
    work = (((0, 1), mom_gu, gu_o, gu_c), ((2,), mom_d, d_o, d_c))
    for place, (kinds, mom, m_o, compact_o) in enumerate(work):
        rows = []
        for kind in kinds:
            own = mine[kind * PAD : (kind + 1) * PAD, :].astype(F32)
            got = theirs[kind * PAD : (kind + 1) * PAD, :].astype(F32)
            rows += [jnp.where(first, own, got), jnp.where(first, got, own)]
        part = mom.shape[1] // len(rows)
        blank = jnp.zeros((n, PAD - part), F32)
        spread = []
        for i in range(len(rows)):
            spread += [mom[:, i * part : (i + 1) * part], blank]
        m = MUON_DECAY * jnp.concatenate(spread, axis=1) + jnp.concatenate(rows, axis=0).T
        m_o[...] = m
        compact_o[...] = compact(m, compact_o.shape[1])
        pieces = []
        for start in range(0, n, 256):
            block = mm(m[start:], m[start : start + 256], NT, HIGH)
            if block.shape[1] == 256:
                pieces += [block[:, :128], block[:, 128:]]
            else:
                pieces.append(jnp.pad(block, ((0, 0), (0, 128 - block.shape[1]))))
        replicas, rows, _ = packed.shape
        rows //= 2
        whole = jnp.concatenate(pieces, axis=0)
        whole = jnp.pad(whole, ((0, replicas * rows - whole.shape[0]), (0, 0)))
        packed[:, place * rows : (place + 1) * rows, :] = whole.reshape(replicas, rows, 128)


def compact(values, width):
    count = values.shape[1] // PAD
    part = width // count
    return jnp.concatenate([values[:, i * PAD : i * PAD + part] for i in range(count)], axis=1)


def muon_large_kernel(scale, packed, m, out):
    n = m.shape[0]
    parts, at = [], 0
    for start in range(0, n, 256):
        rows, cols = n - start, min(256, n - start)
        if cols == 256:
            parts.append(
                jnp.concatenate(
                    [packed[at : at + rows, :], packed[at + rows : at + 2 * rows, :]], axis=1
                )
            )
            at += 2 * rows
        else:
            parts.append(packed[at : at + rows, :cols])
            at += rows
    (x,) = muon_chains([sym_full(parts)], [m[...]])
    out[...] = compact(x * scale, out.shape[1])


def muon_small_kernel(every, m, out, gains):
    count, rows, n = m.shape
    lead = every.shape[1] - gains.shape[0]
    step = lead // count
    grams = []
    for i in range(count):
        whole = every[:, i * step : (i + 1) * step, :].reshape(every.shape[0] * step, n)
        grams.append(mm(whole, whole, TN, HIGH))
    for i, x in enumerate(muon_chains(grams, [m[i].T for i in range(count)])):
        out[i] = x.T
    gains[...] = jnp.sum(every[:, lead:, :], axis=0)


def kernel(body, out_shape, flops, nbytes, vmem=32, **extra):
    return pl.pallas_call(
        body,
        out_shape=out_shape,
        compiler_params=pltpu.CompilerParams(vmem_limit_bytes=vmem * MIB),
        cost_estimate=pl.CostEstimate(flops=flops, bytes_accessed=nbytes, transcendentals=0),
        **extra,
    )


def sds(shape, dtype):
    return jax.ShapeDtypeStruct(shape, dtype)


def in_hbm(value):
    return pltpu.with_memory_space_constraint(value, pltpu.HBM)


def shards(
    tokens,
    cotangent,
    branch,
    w_query,
    w_keyval,
    w_out,
    w_gate_up,
    w_down,
    mom_query,
    mom_keyval,
    mom_out,
    mom_gate_up,
    mom_down,
    norm_gains,
    qk_gains,
    mom_norm,
    mom_qk,
):
    rows, width = tokens.shape
    hd = w_query.shape[3]
    replicas = lax.axis_size("dp")
    half = width // 2
    slab = half // replicas
    cols = w_down.shape[3] // half
    part = cols // 2
    row_index = lax.axis_index("row")
    col_index = lax.axis_index("col")
    me = row_index * 4 + col_index
    first_row = row_index == 0
    row_len = 4 * rows
    rep = 8 * rows

    ff_own = (
        jnp.concatenate(
            [
                w_gate_up.reshape(half, 2, cols).astype(BF).transpose(1, 2, 0),
                w_down.reshape(half, 1, cols).astype(BF).transpose(1, 2, 0),
            ],
            axis=0,
        )
        .reshape(3, 2, part, half)
    )
    ff_keep = jnp.where(first_row, ff_own[:, 0], ff_own[:, 1])
    ff_send = jnp.where(first_row, ff_own[:, 1], ff_own[:, 0])
    ff_send, wq, wk, wo = lax.optimization_barrier((ff_send, w_query, w_keyval, w_out))
    ff_got = flip(ff_send, 4)
    att_own = jnp.concatenate(
        [
            wq.reshape(slab, hd),
            wk[0].reshape(slab, hd),
            wk[1].reshape(slab, hd),
            wo.reshape(hd, slab).T,
        ],
        axis=1,
    ).astype(BF)
    att_other = flip(att_own, 4)
    att_pack = jnp.concatenate(
        [jnp.where(first_row, att_own, att_other), jnp.where(first_row, att_other, att_own)]
    )
    att_shares = jnp.broadcast_to(att_pack[None], (replicas,) + att_pack.shape)
    att_shares, tokens, mom_query, mom_keyval, mom_out, mom_gate_up, mom_down = (
        lax.optimization_barrier(
            (att_shares, tokens, mom_query, mom_keyval, mom_out, mom_gate_up, mom_down)
        )
    )
    ff_pack = jnp.concatenate(
        [jnp.where(first_row, ff_keep, ff_got), jnp.where(first_row, ff_got, ff_keep)], axis=2
    )
    ff_pack = after(jnp.pad(ff_pack, ((0, 0), (0, PAD - part), (0, 0))), att_shares)
    ff_w = lax.all_gather(ff_pack.reshape(3 * PAD, width), "dp", axis=0, tiled=True)
    ff_w = ff_w.reshape(replicas, 3, PAD, width)
    att_all = swap_all(att_shares)
    mom_gu = mom_gate_up.reshape(half, 2 * cols)
    mom_d = mom_down.reshape(half, cols)
    mom_small = jnp.stack(
        [
            mom_query.reshape(slab, hd),
            mom_keyval[0].reshape(slab, hd),
            mom_keyval[1].reshape(slab, hd),
            mom_out.reshape(hd, slab).T,
        ]
    )
    att_all, mom_gu, mom_d, mom_small = lax.optimization_barrier((att_all, mom_gu, mom_d, mom_small))
    slots = jnp.asarray(
        [2 * k + core for pair in (0, 2) for core in (0, 1) for k in (pair, pair + 1)], jnp.int32
    )
    ids = ((me ^ slots)[:, None] * rows + jnp.arange(rows, dtype=jnp.int32)[None, :]).reshape(rep)
    starts = branch[0]
    in_prompt = ids < row_len
    offset = jnp.maximum(ids - row_len, 0)
    segment = jnp.where(in_prompt, -1, offset // CONT_LEN)
    start = jnp.max(
        jnp.where(
            segment[:, None] == jnp.arange(starts.shape[0], dtype=jnp.int32)[None, :],
            starts[None, :],
            0,
        ),
        axis=1,
    )
    position = jnp.where(in_prompt, ids, start + offset % CONT_LEN)
    q_seg, q_pos, q_start = own_rows(segment), own_rows(position), own_rows(start)
    same = (q_seg[:, None] == segment[None, :]) & (position[None, :] <= q_pos[:, None])
    forked = (q_seg[:, None] >= 0) & (segment[None, :] < 0) & (position[None, :] < q_start[:, None])
    seen = (same | forked) & (q_pos[:, None] - position[None, :] < WINDOW)
    mask = jnp.where(seen, 0.0, MASKED).astype(BF)
    steps = jnp.arange(hd // 2, dtype=F32) * (2.0 / hd)
    angle = position.astype(F32)[:, None] * jnp.exp(-math.log(ROPE_BASE) * steps)[None, :]
    cosine, sine = jnp.cos(angle), jnp.sin(angle)

    stream = tokens.astype(F32)
    normed = (stream * inv_rms(stream) * norm_gains[0]).astype(BF)
    normed_all = gather8(normed)
    *attn_parts, att_w, q_raw, k_raw, q, k, v, att, lse = kernel(
        attn_fwd_kernel,
        (sds((rows, width), BF),) * 4
        + (
            pltpu.HBM((width, 4 * hd), BF),
            pltpu.HBM((row_len, hd), F32),
            pltpu.HBM((rep, hd), F32),
            pltpu.HBM((row_len, hd), BF),
            pltpu.HBM((rep, hd), BF),
            pltpu.HBM((rep, hd), BF),
            pltpu.HBM((row_len, hd), BF),
            pltpu.HBM((row_len, 128), F32),
        ),
        3 * 10**9,
        12 * 10**6,
        name="attn_fwd",
    )(*normed_all, att_all, mask, in_hbm(cosine), in_hbm(sine), qk_gains)
    attn_branch = scatter4(attn_parts)
    middle = stream + attn_branch * inv_rms(attn_branch) * norm_gains[1]
    normed_ff = (middle * inv_rms(middle) * norm_gains[2]).astype(BF)

    nf_all = gather8(normed_ff)
    hidden_units = replicas * PAD
    part_spec = pl.BlockSpec((rows, width), lambda i: (0, 0))
    h_out = sds((rep, hidden_units), BF)
    x_out = sds((rows, width), BF)
    rows_all = pltpu.VMEM((rep, width), BF)

    def specs(group):
        return (
            pl.BlockSpec((group, 3, PAD, width), lambda i: (i, 0, 0, 0)),
            pl.BlockSpec((rep, group * PAD), lambda i: (0, i)),
        )

    w_spec, h_spec = specs(4)
    slope, value, hidden, *ff_parts = kernel(
        ffn_fwd_kernel,
        (h_out,) * 3 + (x_out,) * 8,
        8 * 10**9,
        20 * 10**6,
        grid=(replicas // 4,),
        in_specs=[part_spec] * 8 + [w_spec],
        out_specs=[h_spec] * 3 + [part_spec] * 8,
        scratch_shapes=[
            rows_all,
            pltpu.VMEM((replicas // 4, rep, 4 * PAD), BF),
            pltpu.VMEM((hidden_units, width), BF),
        ],
        name="ffn_fwd",
    )(*nf_all, in_hbm(ff_w))
    ff_branch = scatter8(ff_parts)
    layer_out = middle + ff_branch * inv_rms(ff_branch) * norm_gains[3]

    upstream = cotangent.astype(F32)
    ff_grad, grad_post_ff = norm_back(ff_branch, norm_gains[3], upstream)
    df_all = gather8(ff_grad.astype(BF))
    dgate, dup, ff_dw = kernel(
        ffn_units_kernel,
        (pltpu.HBM((rep, hidden_units), BF),) * 2 + (pltpu.HBM((replicas, 3, PAD, width), BF),),
        10 * 10**9,
        30 * 10**6,
        vmem=34,
        grid=(replicas // 8,),
        in_specs=[part_spec] * 16
        + [pl.BlockSpec((8, 1, PAD, width), lambda i: (i, 2, 0, 0))]
        + [specs(8)[1]] * 3,
        out_specs=[specs(8)[1]] * 2 + [specs(8)[0]],
        scratch_shapes=[rows_all, rows_all],
        name="ffn_units",
    )(*nf_all, *df_all, in_hbm(ff_w), slope, value, hidden)
    ff_sum = lax.psum_scatter(
        ff_dw.reshape(replicas * 3 * PAD, width), "dp", scatter_dimension=0, tiled=True
    )
    nf_parts = kernel(
        ffn_tokens_kernel,
        (x_out,) * 8,
        5 * 10**9,
        12 * 10**6,
        grid=(replicas // 8,),
        in_specs=[specs(8)[1]] * 2
        + [pl.BlockSpec((8, 2, PAD, width), lambda i: (i, 0, 0, 0))],
        out_specs=[part_spec] * 8,
        scratch_shapes=[pltpu.VMEM((rep, width), F32)],
        name="ffn_tokens",
    )(in_hbm(dgate), in_hbm(dup), in_hbm(ff_w))
    normed_ff_grad = scatter8(nf_parts)
    middle_part, grad_pre_ff = norm_back(middle, norm_gains[2], normed_ff_grad)
    middle_grad = upstream + middle_part
    attn_grad, grad_post = norm_back(attn_branch, norm_gains[1], middle_grad)

    da_all = gather4(attn_grad.astype(BF))
    *dn_parts, att_dw, grad_qk = kernel(
        attn_bwd_kernel,
        (x_out,) * 8 + (sds((replicas, 2 * slab, 4 * hd), BF), sds((2, hd), F32)),
        6 * 10**9,
        20 * 10**6,
        name="attn_bwd",
    )(*da_all, *normed_all, att_w, mask, cosine, sine, qk_gains, q_raw, k_raw, q, k, v, att, lse)
    att_got = swap_all(att_dw)
    normed_grad = scatter8(dn_parts)
    stream_part, grad_pre = norm_back(stream, norm_gains[0], normed_grad)
    input_grad = middle_grad + stream_part

    flag = row_index.astype(jnp.int32).reshape(1)

    low, high = ff_sum[:, :half], ff_sum[:, half:]
    mine = jnp.where(first_row, low, high)
    swapped = jnp.where(first_row, high, low)
    theirs = flip(swapped, 4)
    share_rows = -(-pack_rows(half) // (8 * replicas)) * 8
    vmem = pl.BlockSpec(memory_space=pltpu.VMEM)
    padded_gu, padded_d, new_gu, new_d, packed = kernel(
        ff_gram_kernel,
        (
            sds((half, 4 * PAD), F32),
            sds((half, 2 * PAD), F32),
            sds((half, 2 * cols), F32),
            sds((half, cols), F32),
            sds((replicas, 2 * share_rows, 128), F32),
        ),
        3 * 10**9,
        6 * 10**6,
        in_specs=[pl.BlockSpec(memory_space=pltpu.SMEM)] + [vmem] * 4,
        name="gram_ff",
    )(flag, mine, theirs, mom_gu, mom_d)
    gram_share = jnp.sum(swap_all(packed), axis=0)
    gram_share = gram_share.reshape(2, -1, 128)

    def everywhere(share):
        return swap_all(jnp.broadcast_to(share[None], (replicas,) + share.shape)).reshape(-1, 128)

    total_gu, total_d = everywhere(gram_share[0]), everywhere(gram_share[1])

    def orthogonal(total, padded, width, name):
        scale = MUON_RATE * math.sqrt(max(1.0, half / (width * replicas)))
        return kernel(
            functools.partial(muon_large_kernel, scale),
            sds((half, width), F32),
            12 * 10**9,
            5 * 10**6,
            name="muon_" + name,
        )(total, padded)

    att_sum = jnp.sum(after(att_got, swapped).astype(F32), axis=0)
    gain_part = jnp.concatenate([grad_pre, grad_post, grad_pre_ff, grad_post_ff], axis=0)
    gain_pack = jnp.concatenate([gain_part.reshape(-1), grad_qk.reshape(-1)])
    gain_rows = gain_pack.shape[0] // (4 * hd)
    gain_pack = gain_pack.reshape(gain_rows, 4 * hd)
    att_lo, att_hi = att_sum[:slab], att_sum[slab:]
    att_g = jnp.concatenate([jnp.where(first_row, att_lo, att_hi), gain_pack]) + flip(
        jnp.concatenate([jnp.where(first_row, att_hi, att_lo), gain_pack]), 4
    )
    ring_g = jnp.concatenate(
        [att_g[:slab, hd : 3 * hd], att_g[slab:].reshape(2 * gain_rows, 2 * hd)], axis=0
    )
    ring_g = ring_g + flip(ring_g, 1)
    ring_g = ring_g + flip(ring_g, 2)
    grad_small = jnp.stack(
        [att_g[:slab, :hd], ring_g[:slab, :hd], ring_g[:slab, hd:], att_g[:slab, 3 * hd :]]
    )
    new_small = MUON_DECAY * mom_small + grad_small
    tile = 8
    slab_rows = -(-slab // tile) * tile
    gains_in = ring_g[slab:].reshape(-1, hd)
    gain_tile = -(-gains_in.shape[0] // tile) * tile
    share = jnp.concatenate(
        [
            jnp.pad(new_small, ((0, 0), (0, slab_rows - slab), (0, 0))).reshape(-1, hd),
            jnp.pad(gains_in, ((0, gain_tile - gains_in.shape[0]), (0, 0))),
        ]
    )
    every = lax.all_gather(share, "dp", axis=0, tiled=True).reshape((replicas,) + share.shape)

    gu_x = orthogonal(total_gu, padded_gu, 2 * cols, "gu")
    d_x = orthogonal(after(total_d, gu_x), padded_d, cols, "down")
    small_x, gain_sum = kernel(
        muon_small_kernel,
        (sds((4, slab, hd), F32), sds((gain_tile, hd), F32)),
        2 * 10**9,
        4 * 10**6,
        name="muon_small",
    )(in_hbm(after(every, d_x)), new_small)
    gain_sum = gain_sum.reshape(-1)
    norm_total = gain_sum[: 4 * width].reshape(4, width)
    qk_total = gain_sum[4 * width : 4 * width + 2 * hd].reshape(2, hd)

    shrink = 1.0 - MUON_RATE * WEIGHT_DECAY
    tall = MUON_RATE * math.sqrt(max(1.0, half / hd))
    flat = MUON_RATE * math.sqrt(max(1.0, hd / half))
    new_query = w_query * shrink - tall * small_x[0].reshape(w_query.shape)
    new_keyval = w_keyval * shrink - tall * small_x[1:3].reshape(w_keyval.shape)
    new_out = w_out * shrink - flat * small_x[3].T.reshape(w_out.shape)
    new_gate_up = w_gate_up * shrink - gu_x.reshape(w_gate_up.shape)
    new_down = w_down * shrink - d_x.reshape(w_down.shape)
    norm_renewed = GAIN_MOMENTUM * mom_norm + norm_total
    qk_renewed = GAIN_MOMENTUM * mom_qk + qk_total
    return (
        layer_out.astype(BF),
        input_grad,
        new_small[0].reshape(mom_query.shape),
        new_query,
        new_query.astype(BF),
        new_small[1:3].reshape(mom_keyval.shape),
        new_keyval,
        new_keyval.astype(BF),
        new_small[3].T.reshape(mom_out.shape),
        new_out,
        new_out.astype(BF),
        new_gu.reshape(mom_gate_up.shape),
        new_gate_up,
        new_gate_up.astype(BF),
        new_d.reshape(mom_down.shape),
        new_down,
        new_down.astype(BF),
        norm_renewed,
        norm_gains - GAIN_RATE * norm_renewed,
        qk_renewed,
        qk_gains - GAIN_RATE * qk_renewed,
    )


def solution(mesh):
    tok = P(("dp", "row", "col"), None)
    query = P("row", "dp", "col", None)
    keyval = P(None, "row", "dp", None)
    out = P("col", None, "row", "dp")
    slabs = P("row", "col", "dp", None)
    weights = (query, keyval, out, slabs, slabs)
    in_specs = (tok, tok, P("dp", None)) + weights + weights + (P(),) * 4
    out_specs = (tok, tok) + tuple(spec for spec in weights for _ in range(3)) + (P(),) * 4
    return jax.shard_map(shards, mesh=mesh, in_specs=in_specs, out_specs=out_specs, check_vma=False)
```

profile of v0, /device:TPU:1, one launch (start us, length us, event | category | flops | bytes accessed | tf_op | source)
XLA Modules:
  0.0 433.8 jit_solution(15786578552734843179)
XLA Ops:
  9.4 2.3 convert_reduce_fusion.1
  14.9 3.7 collective-permute-start
  22.1 3.7 collective-permute-done.18
  27.7 7.9 %all-to-all-start = ((bf16[16,72,1024]{2,1,0:T(8,128)(2,1)}), bf16[16,72,1024]{2,1,0:T(8,128)(2,1)S(1)}, u32[]{:S(2)}, u32[]{:S(2)}) async-start(bf16[16,72,1024]{2,1,0:T(8,128)(2,1)} %broadcast_in_dim.40), calls=%async_computation | async-start | bytes 4718592 | tf_op jit(solution)/shard_map/all_to_all | solution.py:79
  35.8 3.1 multiply_sine_fusion
  39.7 2.4 collective-permute-start.5
  43.1 2.2 select_convert_fusion.refs_9_.refs_13_
  45.3 3.0 collective-permute-start.2
  51.3 3.0 reduce.3
  60.0 12.0 %all-to-all-done.refs_8_ = bf16[16,72,1024]{2,1,0:T(8,128)(2,1)S(1)} async-done(((bf16[16,72,1024]{2,1,0:T(8,128)(2,1)}), bf16[16,72,1024]{2,1,0:T(8,128)(2,1)S(1)}, u32[]{:S(2)}, u32[]{:S(2)}) %all-to-all-start) | async-done | bytes 2359328 | tf_op jit(solution)/shard_map/all_to_all | solution.py:79
  74.2 7.5 %attn_fwd.1 = (bf16[128,1152]{1,0:T(8,128)(2,1)S(1)}, bf16[128,1152]{1,0:T(8,128)(2,1)S(1)}, bf16[128,1152]{1,0:T(8,128)(2,1)S(1)}, bf16[128,1152]{1,0:T(8,128)(...) custom-call(bf16[128,1152]{1,0:T(8,128)(2,1)S(1)} %copy-done.5, ...), custom_call_target="tpu_custom_call" | custom-call | flops 3000000000 | bytes 12000000 | tf_op jit(solution)/shard_map/attn_fwd/pallas_call | solution.py:546
  81.8 4.3 %collective-permute-start.9 = (bf16[128,1152]{1,0:T(8,128)(2,1)S(1)}, bf16[128,1152]{1,0:T(8,128)(2,1)S(1)}, u32[]{:S(2)}, u32[]{:S(2)}) collective-permute-start(bf16[128,1152]{1,0:T(8,128)(2,1)S(1)} %get-tuple-element.105), channel_id=1, source_target_pairs={{0,1},{1,0},{2,3},{3,2},{4,5},{5,4},{6,7},{7,6},{8,9},{9,8},{10,11... | collective-permute-start | bytes 884744 | tf_op jit(solution)/shard_map/ppermute | solution.py:44
  88.3 7.5 %collective-permute-done.10 = bf16[128,1152]{1,0:T(8,128)(2,1)S(1)} collective-permute-done((bf16[128,1152]{1,0:T(8,128)(2,1)S(1)}, bf16[128,1152]{1,0:T(8,128)(2,1)S(1)}, u32[]{:S(2)}, u32[]{:S(2)}) %collective-permute-start.10) | collective-permute-done | bytes 294944 | tf_op jit(solution)/shard_map/ppermute | solution.py:44
  97.8 4.0 collective-permute-start.15
  104.1 10.3 %collective-permute-done.15.refs_5_ = bf16[128,1152]{1,0:T(8,128)(2,1)S(1)} collective-permute-done((bf16[128,1152]{1,0:T(8,128)(2,1)S(1)}, bf16[128,1152]{1,0:T(8,128)(2,1)S(1)}, u32[]{:S(2)}, u32[]{:S(2)}) %collective-permute-start.15) | collective-permute-done | bytes 294944 | tf_op jit(solution)/shard_map/ppermute | solution.py:44
  118.1 13.1 %ffn_fwd.1 = (bf16[1024,1024]{1,0:T(8,128)(2,1)S(1)}, bf16[1024,1024]{1,0:T(8,128)(2,1)S(1)}, bf16[1024,1024]{1,0:T(8,128)(2,1)S(1)}, bf16[128,1152]{1,0:T(8,128...) custom-call(bf16[128,1152]{1,0:T(8,128)(2,1)S(1)} %multiply_convert_, ...), custom_call_target="tpu_custom_call" | custom-call | flops 8000000000 | bytes 20000000 | tf_op jit(solution)/shard_map/ffn_fwd/pallas_call | solution.py:581
  133.0 2.6 collective-permute-start.21
  136.8 6.1 %collective-permute-done.21 = bf16[128,1152]{1,0:T(8,128)(2,1)S(1)} collective-permute-done((bf16[128,1152]{1,0:T(8,128)(2,1)S(1)}, bf16[128,1152]{1,0:T(8,128)(2,1)S(1)}, u32[]{:S(2)}, u32[]{:S(2)}) %collective-permute-start.21) | collective-permute-done | bytes 294944 | tf_op jit(solution)/shard_map/ppermute | solution.py:44
  142.9 7.0 %collective-permute-done.23 = bf16[128,1152]{1,0:T(8,128)(2,1)S(1)} collective-permute-done((bf16[128,1152]{1,0:T(8,128)(2,1)S(1)}, bf16[128,1152]{1,0:T(8,128)(2,1)S(1)}, u32[]{:S(2)}, u32[]{:S(2)}) %collective-permute-start.23) | collective-permute-done | bytes 294944 | tf_op jit(solution)/shard_map/ppermute | solution.py:44
  151.9 2.7 collective-permute-start.30
  156.8 10.5 %collective-permute-done.30.refs_13_ = bf16[128,1152]{1,0:T(8,128)(2,1)S(1)} collective-permute-done((bf16[128,1152]{1,0:T(8,128)(2,1)S(1)}, bf16[128,1152]{1,0:T(8,128)(2,1)S(1)}, u32[]{:S(2)}, u32[]{:S(2)}) %collective-permute-start.30) | collective-permute-done | bytes 294944 | tf_op jit(solution)/shard_map/ppermute | solution.py:44
  168.9 9.2 %collective-permute-start.28 = (bf16[128,1152]{1,0:T(8,128)(2,1)S(1)}, bf16[128,1152]{1,0:T(8,128)(2,1)S(1)}, u32[]{:S(2)}, u32[]{:S(2)}) collective-permute-start(bf16[128,1152]{1,0:T(8,128)(2,1)S(1)} %collective-permute-done.26.refs_9_), channel_id=1, source_target_pairs={{0,1},{1,0},{2,3},{3,2},{4,5},{5,4},{6,7},{7,6},{8,9},{9,8},{10,11... | collective-permute-start | bytes 884744 | tf_op jit(solution)/shard_map/ppermute | solution.py:44
  179.4 15.6 %ffn_units.1 = (bf16[1024,1024]{1,0:T(8,128)(2,1)}, bf16[1024,1024]{1,0:T(8,128)(2,1)}, bf16[16,3,64,1152]{3,2,1,0:T(8,128)(2,1)}) custom-call(bf16[128,1152]{1,0:T(8,128)(2,1)S(1)} %multiply_convert_fusion.refs_0_, bf16[128,1152]{1,0:T(8,128)(2,1)S(1)} %collective-permute-done.11.refs_1_, bf16[128,1152]{1,0:T(8,128)(2,1)S(1)} %collective-permute-done.12.refs_2_, ...), custom_call_target="tpu_custom_call" | custom-call | flops 10000000000 | bytes 30000000 | tf_op jit(solution)/shard_map/ffn_units/pallas_call | solution.py:602
  195.0 8.9 %ffn_tokens.1 = (bf16[128,1152]{1,0:T(8,128)(2,1)S(1)}, bf16[128,1152]{1,0:T(8,128)(2,1)S(1)}, bf16[128,1152]{1,0:T(8,128)(2,1)S(1)}, bf16[128,1152]{1,0:T(8,128...) custom-call(bf16[1024,1024]{1,0:T(8,128)(2,1)} %get-tuple-element.11, ...), custom_call_target="tpu_custom_call" | custom-call | flops 5000000000 | bytes 12000000 | tf_op jit(solution)/shard_map/ffn_tokens/pallas_call | solution.py:619
  209.5 6.2 %collective-permute-done.35 = bf16[128,1152]{1,0:T(8,128)(2,1)S(1)} collective-permute-done((bf16[128,1152]{1,0:T(8,128)(2,1)S(1)}, bf16[128,1152]{1,0:T(8,128)(2,1)S(1)}, u32[]{:S(2)}, u32[]{:S(2)}) %collective-permute-start.35) | collective-permute-done | bytes 294944 | tf_op jit(solution)/shard_map/ppermute | solution.py:44
  215.6 7.0 %collective-permute-done.37 = bf16[128,1152]{1,0:T(8,128)(2,1)S(1)} collective-permute-done((bf16[128,1152]{1,0:T(8,128)(2,1)S(1)}, bf16[128,1152]{1,0:T(8,128)(2,1)S(1)}, u32[]{:S(2)}, u32[]{:S(2)}) %collective-permute-start.37) | collective-permute-done | bytes 294944 | tf_op jit(solution)/shard_map/ppermute | solution.py:44
  226.7 6.5 %collective-permute-done.40.refs_1_ = bf16[128,1152]{1,0:T(8,128)(2,1)S(1)} collective-permute-done((bf16[128,1152]{1,0:T(8,128)(2,1)S(1)}, bf16[128,1152]{1,0:T(8,128)(2,1)S(1)}, u32[]{:S(2)}, u32[]{:S(2)}) %collective-permute-start.40) | collective-permute-done | bytes 294944 | tf_op jit(solution)/shard_map/ppermute | solution.py:44
  236.0 9.7 %attn_bwd.1 = (bf16[128,1152]{1,0:T(8,128)(2,1)S(1)}, bf16[128,1152]{1,0:T(8,128)(2,1)S(1)}, bf16[128,1152]{1,0:T(8,128)(2,1)S(1)}, bf16[128,1152]{1,0:T(8,128)(...) custom-call(bf16[128,1152]{1,0:T(8,128)(2,1)S(1)} %subtract_convert_, ...), custom_call_target="tpu_custom_call" | custom-call | flops 6000000000 | bytes 20000000 | tf_op jit(solution)/shard_map/attn_bwd/pallas_call | solution.py:637
  246.0 4.4 %all-to-all-start.1 = ((bf16[16,72,1024]{2,1,0:T(8,128)(2,1)}), bf16[16,72,1024]{2,1,0:T(8,128)(2,1)}, u32[]{:S(2)}, u32[]{:S(2)}) async-start(bf16[16,72,1024]{2,1,0:T(8,128)(2,1)} %get-tuple-element.146), calls=%async_computation.1 | async-start | bytes 4718592 | tf_op jit(solution)/shard_map/all_to_all | solution.py:79
  252.3 2.5 collective-permute-start.45
  256.0 6.2 %collective-permute-done.45 = bf16[128,1152]{1,0:T(8,128)(2,1)S(1)} collective-permute-done((bf16[128,1152]{1,0:T(8,128)(2,1)S(1)}, bf16[128,1152]{1,0:T(8,128)(2,1)S(1)}, u32[]{:S(2)}, u32[]{:S(2)}) %collective-permute-start.45) | collective-permute-done | bytes 294944 | tf_op jit(solution)/shard_map/ppermute | solution.py:44
  262.2 7.0 %collective-permute-done.47 = bf16[128,1152]{1,0:T(8,128)(2,1)S(1)} collective-permute-done((bf16[128,1152]{1,0:T(8,128)(2,1)S(1)}, bf16[128,1152]{1,0:T(8,128)(2,1)S(1)}, u32[]{:S(2)}, u32[]{:S(2)}) %collective-permute-start.47) | collective-permute-done | bytes 294944 | tf_op jit(solution)/shard_map/ppermute | solution.py:44
  269.7 20.9 %reduce-scatter.2.cloned.1.call-done = bf16[192,1152]{1,0:T(8,128)(2,1)} async-done(((bf16[3072,1152]{1,0:T(8,128)(2,1)}), bf16[192,1152]{1,0:T(8,128)(2,1)}) %reduce-scatter.2.cloned.1.call-update) | async-done | bytes 442384 | tf_op jit(solution)/shard_map/reduce_scatter | solution.py:616
  291.8 2.8 collective-permute-start.53
  296.7 3.7 collective-permute-done.53.theirs
  300.4 3.5 gram_ff.1
  305.4 5.5 %all-to-all-start.2 = ((f32[16,240,128]{2,1,0:T(8,128)}), f32[16,240,128]{2,1,0:T(8,128)}, u32[]{:S(2)}, u32[]{:S(2)}) async-start(f32[16,240,128]{2,1,0:T(8,128)} %get-tuple-element.152), calls=%async_computation.3 | async-start | bytes 3932160 | tf_op jit(solution)/shard_map/all_to_all | solution.py:79
  311.0 3.5 collective-permute-start.50
  314.5 3.4 collective-permute-done.50
  317.9 2.6 collective-permute-start.51
  326.2 10.0 %all-to-all-done.2 = f32[16,240,128]{2,1,0:T(8,128)} async-done(((f32[16,240,128]{2,1,0:T(8,128)}), f32[16,240,128]{2,1,0:T(8,128)}, u32[]{:S(2)}, u32[]{:S(2)}) %all-to-all-start.2) | async-done | bytes 1966112 | tf_op jit(solution)/shard_map/all_to_all | solution.py:79
  338.9 6.9 %all-to-all-start.4 = ((f32[16,120,128]{2,1,0:T(8,128)}), f32[16,120,128]{2,1,0:T(8,128)S(1)}, u32[]{:S(2)}, u32[]{:S(2)}) async-start(f32[16,120,128]{2,1,0:T(8,128)} %broadcast_in_dim.52), calls=%async_computation.5 | async-start | bytes 1966080 | tf_op jit(solution)/shard_map/all_to_all | solution.py:79
  348.7 11.9 %all-to-all-done.4 = f32[16,120,128]{2,1,0:T(8,128)S(1)} async-done(((f32[16,120,128]{2,1,0:T(8,128)}), f32[16,120,128]{2,1,0:T(8,128)S(1)}, u32[]{:S(2)}, u32[]{:S(2)}) %all-to-all-start.4) | async-done | bytes 983072 | tf_op jit(solution)/shard_map/all_to_all | solution.py:79
  361.6 4.7 %all-to-all-start.3 = ((f32[16,120,128]{2,1,0:T(8,128)}), f32[16,120,128]{2,1,0:T(8,128)S(1)}, u32[]{:S(2)}, u32[]{:S(2)}) async-start(f32[16,120,128]{2,1,0:T(8,128)} %broadcast_in_dim.51), calls=%async_computation.4 | async-start | bytes 1966080 | tf_op jit(solution)/shard_map/all_to_all | solution.py:79
  366.3 18.5 %muon_gu.1 = f32[576,216]{1,0:T(8,128)S(1)} custom-call(f32[1920,128]{1,0:T(8,128)S(1)} %bitcast.125, f32[576,256]{1,0:T(8,128)S(1)} %copy-done.17), custom_call_target="tpu_custom_call" | custom-call | flops 12000000000 | bytes 5000000 | tf_op jit(solution)/shard_map/muon_gu/pallas_call | solution.py:681
  385.9 2.9 fusion.34
  388.8 18.6 %muon_down.1 = f32[576,108]{1,0:T(8,128)S(1)} custom-call(f32[1920,128]{1,0:T(8,128)S(1)} %bitcast.126, f32[576,128]{1,0:T(8,128)S(1)} %copy-done.19), custom_call_target="tpu_custom_call" | custom-call | flops 12000000000 | bytes 5000000 | tf_op jit(solution)/shard_map/muon_down/pallas_call | solution.py:681
  409.3 12.7 %muon_small.1 = (f32[4,36,256]{2,1,0:T(8,128)S(1)}, f32[24,256]{1,0:T(8,128)S(1)}) custom-call(f32[16,184,256]{2,1,0:T(8,128)} %bitcast.145, f32[4,36,256]{2,1,0:T(8,128)S(1)} %maximum_add_fusion.m), custom_call_target="tpu_custom_call" | custom-call | flops 2000000000 | bytes 4000000 | tf_op jit(solution)/shard_map/muon_small/pallas_call | solution.py:721
  (346 shorter events, 84.9 us)
Async XLA Ops:
  7.2 110.9 %all-gather.3.cloned.1.call-start = ((), (), s32[]{:S(2)}) async-start(), calls=%async_computation.6 | async-start | bytes 7520256 | tf_op jit(solution)/shard_map/all_gather | solution.py:503
  14.9 5.5 %collective-permute-start = (bf16[36,1024]{1,0:T(8,128)(2,1)S(1)}, bf16[36,1024]{1,0:T(8,128)(2,1)S(1)}, u32[]{:S(2)}, u32[]{:S(2)}) collective-permute-start(bf16[36,1024]{1,0:T(8,128)(2,1)S(1)} %pad_maximum_fusion.6), channel_id=1, source_target_pairs={{0,4},{1,5},{2,6},{3,7},{4,0},{5,1},{6,2},{7,3},{8,12},{9,13},{10,... | collective-permute-start | bytes 221192 | tf_op jit(solution)/shard_map/ppermute | solution.py:44
  18.5 7.4 %collective-permute-start.18 = (bf16[3,54,576]{2,1,0:T(8,128)(2,1)S(1)}, bf16[3,54,576]{2,1,0:T(8,128)(2,1)S(1)}, u32[]{:S(2)}, u32[]{:S(2)}) collective-permute-start(bf16[3,54,576]{2,1,0:T(8,128)(2,1)S(1)} %fusion.21), channel_id=1, source_target_pairs={{0,4},{1,5},{2,6},{3,7},{4,0},{5,1},{6,2},{7,3},{8,12},{9,13},{10,... | collective-permute-start | bytes 559880 | tf_op jit(solution)/shard_map/ppermute | solution.py:44
  27.7 44.3 %all-to-all-start = ((bf16[16,72,1024]{2,1,0:T(8,128)(2,1)}), bf16[16,72,1024]{2,1,0:T(8,128)(2,1)S(1)}, u32[]{:S(2)}, u32[]{:S(2)}) async-start(bf16[16,72,1024]{2,1,0:T(8,128)(2,1)} %broadcast_in_dim.40), calls=%async_computation | async-start | bytes 4718592 | tf_op jit(solution)/shard_map/all_to_all | solution.py:79
  35.7 254.9 %reduce-scatter.2.cloned.1.call-start = ((), (), s32[]{:S(2)}) async-start(), calls=%async_computation.7 | async-start | bytes 7520256 | tf_op jit(solution)/shard_map/reduce_scatter | solution.py:616
  39.7 16.5 %collective-permute-start.5 = (bf16[128,1152]{1,0:T(8,128)(2,1)S(1)}, bf16[128,1152]{1,0:T(8,128)(2,1)}, u32[]{:S(2)}, u32[]{:S(2)}) collective-permute-start(bf16[128,1152]{1,0:T(8,128)(2,1)S(1)} %fusion.12.refs_0_.refs_4_), channel_id=1, source_target_pairs={{0,6},{1,7},{2,4},{3,5},{4,2},{5,3},{6,0},{7,1},{8,14},{9,15},{10,... | collective-permute-start | bytes 884744 | tf_op jit(solution)/shard_map/ppermute | solution.py:44
  42.1 15.0 %collective-permute-start.4 = (bf16[128,1152]{1,0:T(8,128)(2,1)S(1)}, bf16[128,1152]{1,0:T(8,128)(2,1)}, u32[]{:S(2)}, u32[]{:S(2)}) collective-permute-start(bf16[128,1152]{1,0:T(8,128)(2,1)S(1)} %fusion.12.refs_0_.refs_4_), channel_id=1, source_target_pairs={{0,4},{1,5},{2,6},{3,7},{4,0},{5,1},{6,2},{7,3},{8,12},{9,13},{10,... | collective-permute-start | bytes 884744 | tf_op jit(solution)/shard_map/ppermute | solution.py:44
  42.2 15.0 %collective-permute-start.1 = (bf16[128,1152]{1,0:T(8,128)(2,1)S(1)}, bf16[128,1152]{1,0:T(8,128)(2,1)}, u32[]{:S(2)}, u32[]{:S(2)}) collective-permute-start(bf16[128,1152]{1,0:T(8,128)(2,1)S(1)} %fusion.12.refs_0_.refs_4_), channel_id=1, source_target_pairs={{0,2},{1,3},{2,0},{3,1},{4,6},{5,7},{6,4},{7,5},{8,10},{9,11},{10,... | collective-permute-start | bytes 884744 | tf_op jit(solution)/shard_map/ppermute | solution.py:44
  45.3 26.7 %collective-permute-start.2 = (bf16[128,1152]{1,0:T(8,128)(2,1)S(1)}, bf16[128,1152]{1,0:T(8,128)(2,1)}, u32[]{:S(2)}, u32[]{:S(2)}) collective-permute-start(bf16[128,1152]{1,0:T(8,128)(2,1)S(1)} %fusion.12.refs_0_.refs_4_), channel_id=1, source_target_pairs={{0,1},{1,0},{2,3},{3,2},{4,5},{5,4},{6,7},{7,6},{8,9},{9,8},{10,11... | collective-permute-start | bytes 884744 | tf_op jit(solution)/shard_map/ppermute | solution.py:44
  56.2 15.8 %collective-permute-start.7 = (bf16[128,1152]{1,0:T(8,128)(2,1)}, bf16[128,1152]{1,0:T(8,128)(2,1)}, u32[]{:S(2)}, u32[]{:S(2)}) collective-permute-start(bf16[128,1152]{1,0:T(8,128)(2,1)} %collective-permute-done.5.refs_5_.refs_9_), channel_id=1, source_target_pairs={{0,1},{1,0},{2,3},{3,2},{4,5},{5,4},{6,7},{7,6},{8,9},{9,8},{10,11... | collective-permute-start | bytes 884744 | tf_op jit(solution)/shard_map/ppermute | solution.py:44
  57.2 14.8 %collective-permute-start.6 = (bf16[128,1152]{1,0:T(8,128)(2,1)}, bf16[128,1152]{1,0:T(8,128)(2,1)}, u32[]{:S(2)}, u32[]{:S(2)}) collective-permute-start(bf16[128,1152]{1,0:T(8,128)(2,1)} %collective-permute-done.4.refs_4_.refs_8_), channel_id=1, source_target_pairs={{0,1},{1,0},{2,3},{3,2},{4,5},{5,4},{6,7},{7,6},{8,9},{9,8},{10,11... | collective-permute-start | bytes 884744 | tf_op jit(solution)/shard_map/ppermute | solution.py:44
  57.3 14.7 %collective-permute-start.3 = (bf16[128,1152]{1,0:T(8,128)(2,1)}, bf16[128,1152]{1,0:T(8,128)(2,1)}, u32[]{:S(2)}, u32[]{:S(2)}) collective-permute-start(bf16[128,1152]{1,0:T(8,128)(2,1)} %collective-permute-done.1.refs_1_.refs_5_), channel_id=1, source_target_pairs={{0,1},{1,0},{2,3},{3,2},{4,5},{5,4},{6,7},{7,6},{8,9},{9,8},{10,11... | collective-permute-start | bytes 884744 | tf_op jit(solution)/shard_map/ppermute | solution.py:44
  81.8 5.6 %collective-permute-start.9 = (bf16[128,1152]{1,0:T(8,128)(2,1)S(1)}, bf16[128,1152]{1,0:T(8,128)(2,1)S(1)}, u32[]{:S(2)}, u32[]{:S(2)}) collective-permute-start(bf16[128,1152]{1,0:T(8,128)(2,1)S(1)} %get-tuple-element.105), channel_id=1, source_target_pairs={{0,1},{1,0},{2,3},{3,2},{4,5},{5,4},{6,7},{7,6},{8,9},{9,8},{10,11... | collective-permute-start | bytes 884744 | tf_op jit(solution)/shard_map/ppermute | solution.py:44
  87.4 8.4 %collective-permute-start.10 = (bf16[128,1152]{1,0:T(8,128)(2,1)S(1)}, bf16[128,1152]{1,0:T(8,128)(2,1)S(1)}, u32[]{:S(2)}, u32[]{:S(2)}) collective-permute-start(bf16[128,1152]{1,0:T(8,128)(2,1)S(1)} %add_convert_fusion.10), channel_id=1, source_target_pairs={{0,2},{1,3},{2,0},{3,1},{4,6},{5,7},{6,4},{7,5},{8,10},{9,11},{10,... | collective-permute-start | bytes 884744 | tf_op jit(solution)/shard_map/ppermute | solution.py:44
  97.8 16.6 %collective-permute-start.15 = (bf16[128,1152]{1,0:T(8,128)(2,1)S(1)}, bf16[128,1152]{1,0:T(8,128)(2,1)S(1)}, u32[]{:S(2)}, u32[]{:S(2)}) collective-permute-start(bf16[128,1152]{1,0:T(8,128)(2,1)S(1)} %multiply_convert_fusion.refs_0_), channel_id=1, source_target_pairs={{0,6},{1,7},{2,4},{3,5},{4,2},{5,3},{6,0},{7,1},{8,14},{9,15},{10,... | collective-permute-start | bytes 884744 | tf_op jit(solution)/shard_map/ppermute | solution.py:44
  101.8 14.3 %collective-permute-start.14 = (bf16[128,1152]{1,0:T(8,128)(2,1)S(1)}, bf16[128,1152]{1,0:T(8,128)(2,1)S(1)}, u32[]{:S(2)}, u32[]{:S(2)}) collective-permute-start(bf16[128,1152]{1,0:T(8,128)(2,1)S(1)} %multiply_convert_fusion.refs_0_), channel_id=1, source_target_pairs={{0,4},{1,5},{2,6},{3,7},{4,0},{5,1},{6,2},{7,3},{8,12},{9,13},{10,... | collective-permute-start | bytes 884744 | tf_op jit(solution)/shard_map/ppermute | solution.py:44
  101.9 14.2 %collective-permute-start.11 = (bf16[128,1152]{1,0:T(8,128)(2,1)S(1)}, bf16[128,1152]{1,0:T(8,128)(2,1)S(1)}, u32[]{:S(2)}, u32[]{:S(2)}) collective-permute-start(bf16[128,1152]{1,0:T(8,128)(2,1)S(1)} %multiply_convert_fusion.refs_0_), channel_id=1, source_target_pairs={{0,2},{1,3},{2,0},{3,1},{4,6},{5,7},{6,4},{7,5},{8,10},{9,11},{10,... | collective-permute-start | bytes 884744 | tf_op jit(solution)/shard_map/ppermute | solution.py:44
  102.5 14.3 %collective-permute-start.12 = (bf16[128,1152]{1,0:T(8,128)(2,1)S(1)}, bf16[128,1152]{1,0:T(8,128)(2,1)S(1)}, u32[]{:S(2)}, u32[]{:S(2)}) collective-permute-start(bf16[128,1152]{1,0:T(8,128)(2,1)S(1)} %multiply_convert_fusion.refs_0_), channel_id=1, source_target_pairs={{0,1},{1,0},{2,3},{3,2},{4,5},{5,4},{6,7},{7,6},{8,9},{9,8},{10,11... | collective-permute-start | bytes 884744 | tf_op jit(solution)/shard_map/ppermute | solution.py:44
  131.7 5.1 %collective-permute-start.19 = (bf16[128,1152]{1,0:T(8,128)(2,1)S(1)}, bf16[128,1152]{1,0:T(8,128)(2,1)S(1)}, u32[]{:S(2)}, u32[]{:S(2)}) collective-permute-start(bf16[128,1152]{1,0:T(8,128)(2,1)S(1)} %get-tuple-element.109), channel_id=1, source_target_pairs={{0,1},{1,0},{2,3},{3,2},{4,5},{5,4},{6,7},{7,6},{8,9},{9,8},{10,11... | collective-permute-start | bytes 884744 | tf_op jit(solution)/shard_map/ppermute | solution.py:44
  133.0 9.8 %collective-permute-start.21 = (bf16[128,1152]{1,0:T(8,128)(2,1)S(1)}, bf16[128,1152]{1,0:T(8,128)(2,1)S(1)}, u32[]{:S(2)}, u32[]{:S(2)}) collective-permute-start(bf16[128,1152]{1,0:T(8,128)(2,1)S(1)} %add_convert_fusion.9), channel_id=1, source_target_pairs={{0,4},{1,5},{2,6},{3,7},{4,0},{5,1},{6,2},{7,3},{8,12},{9,13},{10,... | collective-permute-start | bytes 884744 | tf_op jit(solution)/shard_map/ppermute | solution.py:44
  135.7 14.2 %collective-permute-start.23 = (bf16[128,1152]{1,0:T(8,128)(2,1)S(1)}, bf16[128,1152]{1,0:T(8,128)(2,1)S(1)}, u32[]{:S(2)}, u32[]{:S(2)}) collective-permute-start(bf16[128,1152]{1,0:T(8,128)(2,1)S(1)} %add_convert_fusion.8), channel_id=1, source_target_pairs={{0,6},{1,7},{2,4},{3,5},{4,2},{5,3},{6,0},{7,1},{8,14},{9,15},{10,... | collective-permute-start | bytes 884744 | tf_op jit(solution)/shard_map/ppermute | solution.py:44
  136.7 13.2 %collective-permute-start.25 = (bf16[128,1152]{1,0:T(8,128)(2,1)S(1)}, bf16[128,1152]{1,0:T(8,128)(2,1)S(1)}, u32[]{:S(2)}, u32[]{:S(2)}) collective-permute-start(bf16[128,1152]{1,0:T(8,128)(2,1)S(1)} %add_convert_fusion.7), channel_id=1, source_target_pairs={{0,2},{1,3},{2,0},{3,1},{4,6},{5,7},{6,4},{7,5},{8,10},{9,11},{10,... | collective-permute-start | bytes 884744 | tf_op jit(solution)/shard_map/ppermute | solution.py:44
  151.9 15.4 %collective-permute-start.30 = (bf16[128,1152]{1,0:T(8,128)(2,1)S(1)}, bf16[128,1152]{1,0:T(8,128)(2,1)S(1)}, u32[]{:S(2)}, u32[]{:S(2)}) collective-permute-start(bf16[128,1152]{1,0:T(8,128)(2,1)S(1)} %get-tuple-element.263.refs_8_), channel_id=1, source_target_pairs={{0,6},{1,7},{2,4},{3,5},{4,2},{5,3},{6,0},{7,1},{8,14},{9,15},{10,... | collective-permute-start | bytes 884744 | tf_op jit(solution)/shard_map/ppermute | solution.py:44
  154.6 14.3 %collective-permute-start.29 = (bf16[128,1152]{1,0:T(8,128)(2,1)S(1)}, bf16[128,1152]{1,0:T(8,128)(2,1)S(1)}, u32[]{:S(2)}, u32[]{:S(2)}) collective-permute-start(bf16[128,1152]{1,0:T(8,128)(2,1)S(1)} %get-tuple-element.263.refs_8_), channel_id=1, source_target_pairs={{0,4},{1,5},{2,6},{3,7},{4,0},{5,1},{6,2},{7,3},{8,12},{9,13},{10,... | collective-permute-start | bytes 884744 | tf_op jit(solution)/shard_map/ppermute | solution.py:44
  154.6 14.3 %collective-permute-start.26 = (bf16[128,1152]{1,0:T(8,128)(2,1)S(1)}, bf16[128,1152]{1,0:T(8,128)(2,1)S(1)}, u32[]{:S(2)}, u32[]{:S(2)}) collective-permute-start(bf16[128,1152]{1,0:T(8,128)(2,1)S(1)} %get-tuple-element.263.refs_8_), channel_id=1, source_target_pairs={{0,2},{1,3},{2,0},{3,1},{4,6},{5,7},{6,4},{7,5},{8,10},{9,11},{10,... | collective-permute-start | bytes 884744 | tf_op jit(solution)/shard_map/ppermute | solution.py:44
  155.2 22.9 %collective-permute-start.27 = (bf16[128,1152]{1,0:T(8,128)(2,1)S(1)}, bf16[128,1152]{1,0:T(8,128)(2,1)S(1)}, u32[]{:S(2)}, u32[]{:S(2)}) collective-permute-start(bf16[128,1152]{1,0:T(8,128)(2,1)S(1)} %get-tuple-element.263.refs_8_), channel_id=1, source_target_pairs={{0,1},{1,0},{2,3},{3,2},{4,5},{5,4},{6,7},{7,6},{8,9},{9,8},{10,11... | collective-permute-start | bytes 884744 | tf_op jit(solution)/shard_map/ppermute | solution.py:44
  167.4 10.7 %collective-permute-start.32 = (bf16[128,1152]{1,0:T(8,128)(2,1)S(1)}, bf16[128,1152]{1,0:T(8,128)(2,1)S(1)}, u32[]{:S(2)}, u32[]{:S(2)}) collective-permute-start(bf16[128,1152]{1,0:T(8,128)(2,1)S(1)} %collective-permute-done.30.refs_13_), channel_id=1, source_target_pairs={{0,1},{1,0},{2,3},{3,2},{4,5},{5,4},{6,7},{7,6},{8,9},{9,8},{10,11... | collective-permute-start | bytes 884744 | tf_op jit(solution)/shard_map/ppermute | solution.py:44
  168.9 9.2 %collective-permute-start.31 = (bf16[128,1152]{1,0:T(8,128)(2,1)S(1)}, bf16[128,1152]{1,0:T(8,128)(2,1)S(1)}, u32[]{:S(2)}, u32[]{:S(2)}) collective-permute-start(bf16[128,1152]{1,0:T(8,128)(2,1)S(1)} %collective-permute-done.29.refs_12_), channel_id=1, source_target_pairs={{0,1},{1,0},{2,3},{3,2},{4,5},{5,4},{6,7},{7,6},{8,9},{9,8},{10,11... | collective-permute-start | bytes 884744 | tf_op jit(solution)/shard_map/ppermute | solution.py:44
  168.9 10.5 %collective-permute-start.28 = (bf16[128,1152]{1,0:T(8,128)(2,1)S(1)}, bf16[128,1152]{1,0:T(8,128)(2,1)S(1)}, u32[]{:S(2)}, u32[]{:S(2)}) collective-permute-start(bf16[128,1152]{1,0:T(8,128)(2,1)S(1)} %collective-permute-done.26.refs_9_), channel_id=1, source_target_pairs={{0,1},{1,0},{2,3},{3,2},{4,5},{5,4},{6,7},{7,6},{8,9},{9,8},{10,11... | collective-permute-start | bytes 884744 | tf_op jit(solution)/shard_map/ppermute | solution.py:44
  204.2 5.2 %collective-permute-start.33 = (bf16[128,1152]{1,0:T(8,128)(2,1)S(1)}, bf16[128,1152]{1,0:T(8,128)(2,1)S(1)}, u32[]{:S(2)}, u32[]{:S(2)}) collective-permute-start(bf16[128,1152]{1,0:T(8,128)(2,1)S(1)} %get-tuple-element.122), channel_id=1, source_target_pairs={{0,1},{1,0},{2,3},{3,2},{4,5},{5,4},{6,7},{7,6},{8,9},{9,8},{10,11... | collective-permute-start | bytes 884744 | tf_op jit(solution)/shard_map/ppermute | solution.py:44
  205.6 10.0 %collective-permute-start.35 = (bf16[128,1152]{1,0:T(8,128)(2,1)S(1)}, bf16[128,1152]{1,0:T(8,128)(2,1)S(1)}, u32[]{:S(2)}, u32[]{:S(2)}) collective-permute-start(bf16[128,1152]{1,0:T(8,128)(2,1)S(1)} %add_convert_fusion.5), channel_id=1, source_target_pairs={{0,4},{1,5},{2,6},{3,7},{4,0},{5,1},{6,2},{7,3},{8,12},{9,13},{10,... | collective-permute-start | bytes 884744 | tf_op jit(solution)/shard_map/ppermute | solution.py:44
  207.8 14.8 %collective-permute-start.37 = (bf16[128,1152]{1,0:T(8,128)(2,1)S(1)}, bf16[128,1152]{1,0:T(8,128)(2,1)S(1)}, u32[]{:S(2)}, u32[]{:S(2)}) collective-permute-start(bf16[128,1152]{1,0:T(8,128)(2,1)S(1)} %add_convert_fusion.4), channel_id=1, source_target_pairs={{0,6},{1,7},{2,4},{3,5},{4,2},{5,3},{6,0},{7,1},{8,14},{9,15},{10,... | collective-permute-start | bytes 884744 | tf_op jit(solution)/shard_map/ppermute | solution.py:44
  209.4 13.2 %collective-permute-start.39 = (bf16[128,1152]{1,0:T(8,128)(2,1)S(1)}, bf16[128,1152]{1,0:T(8,128)(2,1)S(1)}, u32[]{:S(2)}, u32[]{:S(2)}) collective-permute-start(bf16[128,1152]{1,0:T(8,128)(2,1)S(1)} %add_convert_fusion.3), channel_id=1, source_target_pairs={{0,2},{1,3},{2,0},{3,1},{4,6},{5,7},{6,4},{7,5},{8,10},{9,11},{10,... | collective-permute-start | bytes 884744 | tf_op jit(solution)/shard_map/ppermute | solution.py:44
  225.0 8.3 %collective-permute-start.40 = (bf16[128,1152]{1,0:T(8,128)(2,1)S(1)}, bf16[128,1152]{1,0:T(8,128)(2,1)S(1)}, u32[]{:S(2)}, u32[]{:S(2)}) collective-permute-start(bf16[128,1152]{1,0:T(8,128)(2,1)S(1)} %subtract_convert_fusion.refs_0_), channel_id=1, source_target_pairs={{0,2},{1,3},{2,0},{3,1},{4,6},{5,7},{6,4},{7,5},{8,10},{9,11},{10,... | collective-permute-start | bytes 884744 | tf_op jit(solution)/shard_map/ppermute | solution.py:44
  226.0 8.6 %collective-permute-start.41 = (bf16[128,1152]{1,0:T(8,128)(2,1)S(1)}, bf16[128,1152]{1,0:T(8,128)(2,1)S(1)}, u32[]{:S(2)}, u32[]{:S(2)}) collective-permute-start(bf16[128,1152]{1,0:T(8,128)(2,1)S(1)} %subtract_convert_fusion.refs_0_), channel_id=1, source_target_pairs={{0,1},{1,0},{2,3},{3,2},{4,5},{5,4},{6,7},{7,6},{8,9},{9,8},{10,11... | collective-permute-start | bytes 884744 | tf_op jit(solution)/shard_map/ppermute | solution.py:44
  245.6 5.6 %collective-permute-start.44 = (bf16[128,1152]{1,0:T(8,128)(2,1)S(1)}, bf16[128,1152]{1,0:T(8,128)(2,1)}, u32[]{:S(2)}, u32[]{:S(2)}) collective-permute-start(bf16[128,1152]{1,0:T(8,128)(2,1)S(1)} %get-tuple-element.140), channel_id=1, source_target_pairs={{0,1},{1,0},{2,3},{3,2},{4,5},{5,4},{6,7},{7,6},{8,9},{9,8},{10,11... | collective-permute-start | bytes 884744 | tf_op jit(solution)/shard_map/ppermute | solution.py:44
  246.0 48.5 %all-to-all-start.1 = ((bf16[16,72,1024]{2,1,0:T(8,128)(2,1)}), bf16[16,72,1024]{2,1,0:T(8,128)(2,1)}, u32[]{:S(2)}, u32[]{:S(2)}) async-start(bf16[16,72,1024]{2,1,0:T(8,128)(2,1)} %get-tuple-element.146), calls=%async_computation.1 | async-start | bytes 4718592 | tf_op jit(solution)/shard_map/all_to_all | solution.py:79
  250.5 5.5 %collective-permute-start.43 = (bf16[128,1152]{1,0:T(8,128)(2,1)S(1)}, bf16[128,1152]{1,0:T(8,128)(2,1)S(1)}, u32[]{:S(2)}, u32[]{:S(2)}) collective-permute-start(bf16[128,1152]{1,0:T(8,128)(2,1)S(1)} %get-tuple-element.138), channel_id=1, source_target_pairs={{0,1},{1,0},{2,3},{3,2},{4,5},{5,4},{6,7},{7,6},{8,9},{9,8},{10,11... | collective-permute-start | bytes 884744 | tf_op jit(solution)/shard_map/ppermute | solution.py:44
  251.1 4.6 %collective-permute-start.48 = (bf16[128,1152]{1,0:T(8,128)(2,1)S(1)}, bf16[128,1152]{1,0:T(8,128)(2,1)S(1)}, u32[]{:S(2)}, u32[]{:S(2)}) collective-permute-start(bf16[128,1152]{1,0:T(8,128)(2,1)S(1)} %get-tuple-element.144), channel_id=1, source_target_pairs={{0,1},{1,0},{2,3},{3,2},{4,5},{5,4},{6,7},{7,6},{8,9},{9,8},{10,11... | collective-permute-start | bytes 884744 | tf_op jit(solution)/shard_map/ppermute | solution.py:44
  252.3 9.9 %collective-permute-start.45 = (bf16[128,1152]{1,0:T(8,128)(2,1)S(1)}, bf16[128,1152]{1,0:T(8,128)(2,1)S(1)}, u32[]{:S(2)}, u32[]{:S(2)}) collective-permute-start(bf16[128,1152]{1,0:T(8,128)(2,1)S(1)} %add_convert_fusion.2), channel_id=1, source_target_pairs={{0,4},{1,5},{2,6},{3,7},{4,0},{5,1},{6,2},{7,3},{8,12},{9,13},{10,... | collective-permute-start | bytes 884744 | tf_op jit(solution)/shard_map/ppermute | solution.py:44
  254.8 14.4 %collective-permute-start.47 = (bf16[128,1152]{1,0:T(8,128)(2,1)S(1)}, bf16[128,1152]{1,0:T(8,128)(2,1)S(1)}, u32[]{:S(2)}, u32[]{:S(2)}) collective-permute-start(bf16[128,1152]{1,0:T(8,128)(2,1)S(1)} %add_convert_fusion.1), channel_id=1, source_target_pairs={{0,6},{1,7},{2,4},{3,5},{4,2},{5,3},{6,0},{7,1},{8,14},{9,15},{10,... | collective-permute-start | bytes 884744 | tf_op jit(solution)/shard_map/ppermute | solution.py:44
  255.8 13.5 %collective-permute-start.49 = (bf16[128,1152]{1,0:T(8,128)(2,1)S(1)}, bf16[128,1152]{1,0:T(8,128)(2,1)S(1)}, u32[]{:S(2)}, u32[]{:S(2)}) collective-permute-start(bf16[128,1152]{1,0:T(8,128)(2,1)S(1)} %add_convert_fusion), channel_id=1, source_target_pairs={{0,2},{1,3},{2,0},{3,1},{4,6},{5,7},{6,4},{7,5},{8,10},{9,11},{10,... | collective-permute-start | bytes 884744 | tf_op jit(solution)/shard_map/ppermute | solution.py:44
  291.8 8.6 %collective-permute-start.53 = (bf16[192,576]{1,0:T(8,128)(2,1)S(1)}, bf16[192,576]{1,0:T(8,128)(2,1)S(1)}, u32[]{:S(2)}, u32[]{:S(2)}) collective-permute-start(bf16[192,576]{1,0:T(8,128)(2,1)S(1)} %get-tuple-element.266), channel_id=1, source_target_pairs={{0,4},{1,5},{2,6},{3,7},{4,0},{5,1},{6,2},{7,3},{8,12},{9,13},{10,... | collective-permute-start | bytes 663560 | tf_op jit(solution)/shard_map/ppermute | solution.py:44
  305.4 30.7 %all-to-all-start.2 = ((f32[16,240,128]{2,1,0:T(8,128)}), f32[16,240,128]{2,1,0:T(8,128)}, u32[]{:S(2)}, u32[]{:S(2)}) async-start(f32[16,240,128]{2,1,0:T(8,128)} %get-tuple-element.152), calls=%async_computation.3 | async-start | bytes 3932160 | tf_op jit(solution)/shard_map/all_to_all | solution.py:79
  311.0 6.9 %collective-permute-start.50 = (f32[41,1024]{1,0:T(8,128)S(1)}, f32[41,1024]{1,0:T(8,128)S(1)}, u32[]{:S(2)}, u32[]{:S(2)}) collective-permute-start(f32[41,1024]{1,0:T(8,128)S(1)} %pad_maximum_fusion.1), channel_id=1, source_target_pairs={{0,4},{1,5},{2,6},{3,7},{4,0},{5,1},{6,2},{7,3},{8,12},{9,13},{10,... | collective-permute-start | bytes 503816 | tf_op jit(solution)/shard_map/ppermute | solution.py:44
  338.9 21.7 %all-to-all-start.4 = ((f32[16,120,128]{2,1,0:T(8,128)}), f32[16,120,128]{2,1,0:T(8,128)S(1)}, u32[]{:S(2)}, u32[]{:S(2)}) async-start(f32[16,120,128]{2,1,0:T(8,128)} %broadcast_in_dim.52), calls=%async_computation.5 | async-start | bytes 1966080 | tf_op jit(solution)/shard_map/all_to_all | solution.py:79
  345.8 63.4 %all-gather.5.cloned.1.call-start = ((), (), s32[]{:S(2)}) async-start(), calls=%async_computation.8 | async-start | bytes 3203072 | tf_op jit(solution)/shard_map/all_gather | solution.py:717
  361.6 27.2 %all-to-all-start.3 = ((f32[16,120,128]{2,1,0:T(8,128)}), f32[16,120,128]{2,1,0:T(8,128)S(1)}, u32[]{:S(2)}, u32[]{:S(2)}) async-start(f32[16,120,128]{2,1,0:T(8,128)} %broadcast_in_dim.51), calls=%async_computation.4 | async-start | bytes 1966080 | tf_op jit(solution)/shard_map/all_to_all | solution.py:79
  (82 other events, 956.9 us)
Sparse Core Ops, SparseCore 0:
  27.0 86.3 all-gather.2
  195.1 95.4 reduce-scatter.1
  349.0 58.2 all-gather.4
where the time goes:
time: 441 us; the launch traced here: 434 us
  waiting for transfers between devices  148 us (34%)
  Pallas kernels  108 us (24%)
  starting transfers between devices  98 us (22%)
  other arithmetic  38.9 us (9%)
  local copies, waits for them, and re-layouts  25.9 us (6%)
  between operations  15.2 us (3%)
    ppermute x54, waiting for transfers between devices, flip(): return lax.ppermute(block, RING, [(i, i ^ bits) for i in range(8)])  92.9 us
    ppermute x54, starting transfers between devices, flip(): return lax.ppermute(block, RING, [(i, i ^ bits) for i in range(8)])  68.6 us
    pallas_call x2, Pallas kernels, orthogonal(): kernel(functools.partial(muon_large_kernel, scale), sds((half, width), F3...  37.2 us
    all_to_all x5, waiting for transfers between devices, swap_all(): return lax.all_to_all(blocks, 'dp', 0, 0, tiled=True)  33.9 us
    all_to_all x5, starting transfers between devices, swap_all(): return lax.all_to_all(blocks, 'dp', 0, 0, tiled=True)  29.3 us
    reduce_scatter x1, waiting for transfers between devices, shards(): lax.psum_scatter(ff_dw.reshape(replicas * 3 * PAD, width), 'dp', scatter_...  20.9 us
    pallas_call x1, Pallas kernels, shards(): kernel(ffn_units_kernel, (pltpu.HBM((rep, hidden_units), BF),) * 2 + (plt...  15.6 us
    pallas_call x1, Pallas kernels, shards(): kernel(ffn_fwd_kernel, (h_out,) * 3 + (x_out,) * 8, 8 * 10 ** 9, 20 * 10...  13.1 us
  transfers between devices with their start and end apart: 62, of which 26 were waited for; matrix products, arithmetic and copies ran while one was open for 10% of the time, Pallas kernels for 15%

commit v1 on v0

--- a/solution.py
+++ b/solution.py
@@ -559,7 +559,7 @@
         3 * 10**9,
         12 * 10**6,
         name="attn_fwd",
-    )(*normed_all, att_all, mask, in_hbm(cosine), in_hbm(sine), qk_gains)
+    )(in_hbm(normed_all[0]), *normed_all[1:], att_all, in_hbm(mask), in_hbm(cosine), in_hbm(sine), qk_gains)
     attn_branch = scatter4(attn_parts)
     middle = stream + attn_branch * inv_rms(attn_branch) * norm_gains[1]
     normed_ff = (middle * inv_rms(middle) * norm_gains[2]).astype(BF)

time: 441 us -> 439 us (level)
    unnamed x145 -> x141, local copies, waits for them, and re-layouts: 9.6 us -> 7.4 us
  transfers between devices with their start and end apart: 62 -> 62, of which waited for: 26 -> 27; matrix products, arithmetic and copies ran while one was open for 10% -> 10% of each run, Pallas kernels for 15% -> 15%
where the time goes in v1:
time: 439 us; the launch traced here: 433 us
  waiting for transfers between devices  151 us (34%)
  Pallas kernels  108 us (25%)
  starting transfers between devices  96.5 us (22%)
  other arithmetic  38.8 us (9%)
  local copies, waits for them, and re-layouts  23.7 us (5%)
  between operations  15.2 us (3%)
    ppermute x54, waiting for transfers between devices, flip(): return lax.ppermute(block, RING, [(i, i ^ bits) for i in range(8)])  93.8 us
    ppermute x54, starting transfers between devices, flip(): return lax.ppermute(block, RING, [(i, i ^ bits) for i in range(8)])  67 us
    pallas_call x2, Pallas kernels, orthogonal(): kernel(functools.partial(muon_large_kernel, scale), sds((half, width), F3...  37.2 us
    all_to_all x5, waiting for transfers between devices, swap_all(): return lax.all_to_all(blocks, 'dp', 0, 0, tiled=True)  36 us
    all_to_all x5, starting transfers between devices, swap_all(): return lax.all_to_all(blocks, 'dp', 0, 0, tiled=True)  29.4 us
    reduce_scatter x1, waiting for transfers between devices, shards(): lax.psum_scatter(ff_dw.reshape(replicas * 3 * PAD, width), 'dp', scatter_...  20.8 us
    pallas_call x1, Pallas kernels, shards(): kernel(ffn_units_kernel, (pltpu.HBM((rep, hidden_units), BF),) * 2 + (plt...  15.6 us
    pallas_call x1, Pallas kernels, shards(): kernel(ffn_fwd_kernel, (h_out,) * 3 + (x_out,) * 8, 8 * 10 ** 9, 20 * 10...  13.1 us
  transfers between devices with their start and end apart: 62, of which 27 were waited for; matrix products, arithmetic and copies ran while one was open for 10% of the time, Pallas kernels for 15%

profile of v1, /device:TPU:1, one launch (start us, length us, event | category | flops | bytes accessed | tf_op | source)
XLA Modules:
  0.0 433.1 jit_solution(15025423755596552878)
XLA Ops:
  9.4 2.3 convert_reduce_fusion.1
  14.9 3.7 collective-permute-start
  22.2 3.7 collective-permute-done.18
  27.7 7.9 %all-to-all-start = ((bf16[16,72,1024]{2,1,0:T(8,128)(2,1)}), bf16[16,72,1024]{2,1,0:T(8,128)(2,1)S(1)}, u32[]{:S(2)}, u32[]{:S(2)}) async-start(bf16[16,72,1024]{2,1,0:T(8,128)(2,1)} %broadcast_in_dim.40), calls=%async_computation | async-start | bytes 4718592 | tf_op jit(solution)/shard_map/all_to_all | solution.py:79
  35.8 3.1 multiply_sine_fusion
  39.7 2.4 collective-permute-start.5
  43.1 2.2 select_convert_fusion.refs_9_.refs_13_
  45.3 3.0 collective-permute-start.2
  51.3 3.0 reduce.3
  60.0 12.1 %all-to-all-done.refs_8_ = bf16[16,72,1024]{2,1,0:T(8,128)(2,1)S(1)} async-done(((bf16[16,72,1024]{2,1,0:T(8,128)(2,1)}), bf16[16,72,1024]{2,1,0:T(8,128)(2,1)S(1)}, u32[]{:S(2)}, u32[]{:S(2)}) %all-to-all-start) | async-done | bytes 2359328 | tf_op jit(solution)/shard_map/all_to_all | solution.py:79
  72.1 7.6 %attn_fwd.1 = (bf16[128,1152]{1,0:T(8,128)(2,1)S(1)}, bf16[128,1152]{1,0:T(8,128)(2,1)S(1)}, bf16[128,1152]{1,0:T(8,128)(2,1)S(1)}, bf16[128,1152]{1,0:T(8,128)(...) custom-call(bf16[128,1152]{1,0:T(8,128)(2,1)} %copy-done.3, ...), custom_call_target="tpu_custom_call" | custom-call | flops 3000000000 | bytes 12000000 | tf_op jit(solution)/shard_map/attn_fwd/pallas_call | solution.py:546
  79.7 4.4 %collective-permute-start.9 = (bf16[128,1152]{1,0:T(8,128)(2,1)S(1)}, bf16[128,1152]{1,0:T(8,128)(2,1)S(1)}, u32[]{:S(2)}, u32[]{:S(2)}) collective-permute-start(bf16[128,1152]{1,0:T(8,128)(2,1)S(1)} %get-tuple-element.105), channel_id=1, source_target_pairs={{0,1},{1,0},{2,3},{3,2},{4,5},{5,4},{6,7},{7,6},{8,9},{9,8},{10,11... | collective-permute-start | bytes 884744 | tf_op jit(solution)/shard_map/ppermute | solution.py:44
  86.3 7.5 %collective-permute-done.10 = bf16[128,1152]{1,0:T(8,128)(2,1)S(1)} collective-permute-done((bf16[128,1152]{1,0:T(8,128)(2,1)S(1)}, bf16[128,1152]{1,0:T(8,128)(2,1)S(1)}, u32[]{:S(2)}, u32[]{:S(2)}) %collective-permute-start.10) | collective-permute-done | bytes 294944 | tf_op jit(solution)/shard_map/ppermute | solution.py:44
  95.8 4.0 collective-permute-start.15
  102.1 10.3 %collective-permute-done.15.refs_5_ = bf16[128,1152]{1,0:T(8,128)(2,1)S(1)} collective-permute-done((bf16[128,1152]{1,0:T(8,128)(2,1)S(1)}, bf16[128,1152]{1,0:T(8,128)(2,1)S(1)}, u32[]{:S(2)}, u32[]{:S(2)}) %collective-permute-start.15) | collective-permute-done | bytes 294944 | tf_op jit(solution)/shard_map/ppermute | solution.py:44
  116.1 13.1 %ffn_fwd.1 = (bf16[1024,1024]{1,0:T(8,128)(2,1)S(1)}, bf16[1024,1024]{1,0:T(8,128)(2,1)S(1)}, bf16[1024,1024]{1,0:T(8,128)(2,1)S(1)}, bf16[128,1152]{1,0:T(8,128...) custom-call(bf16[128,1152]{1,0:T(8,128)(2,1)S(1)} %multiply_convert_, ...), custom_call_target="tpu_custom_call" | custom-call | flops 8000000000 | bytes 20000000 | tf_op jit(solution)/shard_map/ffn_fwd/pallas_call | solution.py:581
  131.0 2.6 collective-permute-start.21
  134.8 6.1 %collective-permute-done.21 = bf16[128,1152]{1,0:T(8,128)(2,1)S(1)} collective-permute-done((bf16[128,1152]{1,0:T(8,128)(2,1)S(1)}, bf16[128,1152]{1,0:T(8,128)(2,1)S(1)}, u32[]{:S(2)}, u32[]{:S(2)}) %collective-permute-start.21) | collective-permute-done | bytes 294944 | tf_op jit(solution)/shard_map/ppermute | solution.py:44
  140.8 7.0 %collective-permute-done.23 = bf16[128,1152]{1,0:T(8,128)(2,1)S(1)} collective-permute-done((bf16[128,1152]{1,0:T(8,128)(2,1)S(1)}, bf16[128,1152]{1,0:T(8,128)(2,1)S(1)}, u32[]{:S(2)}, u32[]{:S(2)}) %collective-permute-start.23) | collective-permute-done | bytes 294944 | tf_op jit(solution)/shard_map/ppermute | solution.py:44
  149.9 2.7 collective-permute-start.30
  154.8 10.5 %collective-permute-done.30.refs_13_ = bf16[128,1152]{1,0:T(8,128)(2,1)S(1)} collective-permute-done((bf16[128,1152]{1,0:T(8,128)(2,1)S(1)}, bf16[128,1152]{1,0:T(8,128)(2,1)S(1)}, u32[]{:S(2)}, u32[]{:S(2)}) %collective-permute-start.30) | collective-permute-done | bytes 294944 | tf_op jit(solution)/shard_map/ppermute | solution.py:44
  166.9 9.2 %collective-permute-start.28 = (bf16[128,1152]{1,0:T(8,128)(2,1)S(1)}, bf16[128,1152]{1,0:T(8,128)(2,1)S(1)}, u32[]{:S(2)}, u32[]{:S(2)}) collective-permute-start(bf16[128,1152]{1,0:T(8,128)(2,1)S(1)} %collective-permute-done.26.refs_9_), channel_id=1, source_target_pairs={{0,1},{1,0},{2,3},{3,2},{4,5},{5,4},{6,7},{7,6},{8,9},{9,8},{10,11... | collective-permute-start | bytes 884744 | tf_op jit(solution)/shard_map/ppermute | solution.py:44
  177.3 15.6 %ffn_units.1 = (bf16[1024,1024]{1,0:T(8,128)(2,1)}, bf16[1024,1024]{1,0:T(8,128)(2,1)}, bf16[16,3,64,1152]{3,2,1,0:T(8,128)(2,1)}) custom-call(bf16[128,1152]{1,0:T(8,128)(2,1)S(1)} %multiply_convert_fusion.refs_0_, bf16[128,1152]{1,0:T(8,128)(2,1)S(1)} %collective-permute-done.11.refs_1_, bf16[128,1152]{1,0:T(8,128)(2,1)S(1)} %collective-permute-done.12.refs_2_, ...), custom_call_target="tpu_custom_call" | custom-call | flops 10000000000 | bytes 30000000 | tf_op jit(solution)/shard_map/ffn_units/pallas_call | solution.py:602
  193.0 8.9 %ffn_tokens.1 = (bf16[128,1152]{1,0:T(8,128)(2,1)S(1)}, bf16[128,1152]{1,0:T(8,128)(2,1)S(1)}, bf16[128,1152]{1,0:T(8,128)(2,1)S(1)}, bf16[128,1152]{1,0:T(8,128...) custom-call(bf16[1024,1024]{1,0:T(8,128)(2,1)} %get-tuple-element.11, ...), custom_call_target="tpu_custom_call" | custom-call | flops 5000000000 | bytes 12000000 | tf_op jit(solution)/shard_map/ffn_tokens/pallas_call | solution.py:619
  207.4 6.1 %collective-permute-done.35 = bf16[128,1152]{1,0:T(8,128)(2,1)S(1)} collective-permute-done((bf16[128,1152]{1,0:T(8,128)(2,1)S(1)}, bf16[128,1152]{1,0:T(8,128)(2,1)S(1)}, u32[]{:S(2)}, u32[]{:S(2)}) %collective-permute-start.35) | collective-permute-done | bytes 294944 | tf_op jit(solution)/shard_map/ppermute | solution.py:44
  213.6 7.0 %collective-permute-done.37 = bf16[128,1152]{1,0:T(8,128)(2,1)S(1)} collective-permute-done((bf16[128,1152]{1,0:T(8,128)(2,1)S(1)}, bf16[128,1152]{1,0:T(8,128)(2,1)S(1)}, u32[]{:S(2)}, u32[]{:S(2)}) %collective-permute-start.37) | collective-permute-done | bytes 294944 | tf_op jit(solution)/shard_map/ppermute | solution.py:44
  224.7 6.4 %collective-permute-done.40.refs_1_ = bf16[128,1152]{1,0:T(8,128)(2,1)S(1)} collective-permute-done((bf16[128,1152]{1,0:T(8,128)(2,1)S(1)}, bf16[128,1152]{1,0:T(8,128)(2,1)S(1)}, u32[]{:S(2)}, u32[]{:S(2)}) %collective-permute-start.40) | collective-permute-done | bytes 294944 | tf_op jit(solution)/shard_map/ppermute | solution.py:44
  233.9 9.7 %attn_bwd.1 = (bf16[128,1152]{1,0:T(8,128)(2,1)S(1)}, bf16[128,1152]{1,0:T(8,128)(2,1)S(1)}, bf16[128,1152]{1,0:T(8,128)(2,1)S(1)}, bf16[128,1152]{1,0:T(8,128)(...) custom-call(bf16[128,1152]{1,0:T(8,128)(2,1)S(1)} %subtract_convert_, ...), custom_call_target="tpu_custom_call" | custom-call | flops 6000000000 | bytes 20000000 | tf_op jit(solution)/shard_map/attn_bwd/pallas_call | solution.py:637
  244.0 4.4 %all-to-all-start.1 = ((bf16[16,72,1024]{2,1,0:T(8,128)(2,1)}), bf16[16,72,1024]{2,1,0:T(8,128)(2,1)}, u32[]{:S(2)}, u32[]{:S(2)}) async-start(bf16[16,72,1024]{2,1,0:T(8,128)(2,1)} %get-tuple-element.146), calls=%async_computation.1 | async-start | bytes 4718592 | tf_op jit(solution)/shard_map/all_to_all | solution.py:79
  250.3 2.5 collective-permute-start.45
  254.0 6.2 %collective-permute-done.45 = bf16[128,1152]{1,0:T(8,128)(2,1)S(1)} collective-permute-done((bf16[128,1152]{1,0:T(8,128)(2,1)S(1)}, bf16[128,1152]{1,0:T(8,128)(2,1)S(1)}, u32[]{:S(2)}, u32[]{:S(2)}) %collective-permute-start.45) | collective-permute-done | bytes 294944 | tf_op jit(solution)/shard_map/ppermute | solution.py:44
  260.2 7.0 %collective-permute-done.47 = bf16[128,1152]{1,0:T(8,128)(2,1)S(1)} collective-permute-done((bf16[128,1152]{1,0:T(8,128)(2,1)S(1)}, bf16[128,1152]{1,0:T(8,128)(2,1)S(1)}, u32[]{:S(2)}, u32[]{:S(2)}) %collective-permute-start.47) | collective-permute-done | bytes 294944 | tf_op jit(solution)/shard_map/ppermute | solution.py:44
  267.7 20.8 %reduce-scatter.2.cloned.1.call-done = bf16[192,1152]{1,0:T(8,128)(2,1)} async-done(((bf16[3072,1152]{1,0:T(8,128)(2,1)}), bf16[192,1152]{1,0:T(8,128)(2,1)}) %reduce-scatter.2.cloned.1.call-update) | async-done | bytes 442384 | tf_op jit(solution)/shard_map/reduce_scatter | solution.py:616
  289.7 2.8 collective-permute-start.53
  294.6 3.5 collective-permute-done.53.theirs
  298.1 3.5 gram_ff.1
  303.2 6.8 %all-to-all-start.2 = ((f32[16,240,128]{2,1,0:T(8,128)}), f32[16,240,128]{2,1,0:T(8,128)}, u32[]{:S(2)}, u32[]{:S(2)}) async-start(f32[16,240,128]{2,1,0:T(8,128)} %get-tuple-element.152), calls=%async_computation.3 | async-start | bytes 3932160 | tf_op jit(solution)/shard_map/all_to_all | solution.py:79
  310.1 2.4 collective-permute-start.50
  312.5 4.0 collective-permute-done.50
  316.6 2.5 collective-permute-start.51
  324.7 12.1 %all-to-all-done.2 = f32[16,240,128]{2,1,0:T(8,128)} async-done(((f32[16,240,128]{2,1,0:T(8,128)}), f32[16,240,128]{2,1,0:T(8,128)}, u32[]{:S(2)}, u32[]{:S(2)}) %all-to-all-start.2) | async-done | bytes 1966112 | tf_op jit(solution)/shard_map/all_to_all | solution.py:79
  339.5 5.6 %all-to-all-start.4 = ((f32[16,120,128]{2,1,0:T(8,128)}), f32[16,120,128]{2,1,0:T(8,128)S(1)}, u32[]{:S(2)}, u32[]{:S(2)}) async-start(f32[16,120,128]{2,1,0:T(8,128)} %broadcast_in_dim.52), calls=%async_computation.5 | async-start | bytes 1966080 | tf_op jit(solution)/shard_map/all_to_all | solution.py:79
  347.9 11.9 %all-to-all-done.4 = f32[16,120,128]{2,1,0:T(8,128)S(1)} async-done(((f32[16,120,128]{2,1,0:T(8,128)}), f32[16,120,128]{2,1,0:T(8,128)S(1)}, u32[]{:S(2)}, u32[]{:S(2)}) %all-to-all-start.4) | async-done | bytes 983072 | tf_op jit(solution)/shard_map/all_to_all | solution.py:79
  360.9 4.7 %all-to-all-start.3 = ((f32[16,120,128]{2,1,0:T(8,128)}), f32[16,120,128]{2,1,0:T(8,128)S(1)}, u32[]{:S(2)}, u32[]{:S(2)}) async-start(f32[16,120,128]{2,1,0:T(8,128)} %broadcast_in_dim.51), calls=%async_computation.4 | async-start | bytes 1966080 | tf_op jit(solution)/shard_map/all_to_all | solution.py:79
  365.6 18.5 %muon_gu.1 = f32[576,216]{1,0:T(8,128)S(1)} custom-call(f32[1920,128]{1,0:T(8,128)S(1)} %bitcast.125, f32[576,256]{1,0:T(8,128)S(1)} %copy-done.15), custom_call_target="tpu_custom_call" | custom-call | flops 12000000000 | bytes 5000000 | tf_op jit(solution)/shard_map/muon_gu/pallas_call | solution.py:681
  385.2 2.9 fusion.34
  388.1 18.6 %muon_down.1 = f32[576,108]{1,0:T(8,128)S(1)} custom-call(f32[1920,128]{1,0:T(8,128)S(1)} %bitcast.126, f32[576,128]{1,0:T(8,128)S(1)} %copy-done.17), custom_call_target="tpu_custom_call" | custom-call | flops 12000000000 | bytes 5000000 | tf_op jit(solution)/shard_map/muon_down/pallas_call | solution.py:681
  408.5 12.7 %muon_small.1 = (f32[4,36,256]{2,1,0:T(8,128)S(1)}, f32[24,256]{1,0:T(8,128)S(1)}) custom-call(f32[16,184,256]{2,1,0:T(8,128)} %bitcast.145, f32[4,36,256]{2,1,0:T(8,128)S(1)} %maximum_add_fusion.m), custom_call_target="tpu_custom_call" | custom-call | flops 2000000000 | bytes 4000000 | tf_op jit(solution)/shard_map/muon_small/pallas_call | solution.py:721
  (342 shorter events, 82.6 us)
Async XLA Ops:
  7.2 108.9 %all-gather.3.cloned.1.call-start = ((), (), s32[]{:S(2)}) async-start(), calls=%async_computation.6 | async-start | bytes 7520256 | tf_op jit(solution)/shard_map/all_gather | solution.py:503
  14.9 5.5 %collective-permute-start = (bf16[36,1024]{1,0:T(8,128)(2,1)S(1)}, bf16[36,1024]{1,0:T(8,128)(2,1)S(1)}, u32[]{:S(2)}, u32[]{:S(2)}) collective-permute-start(bf16[36,1024]{1,0:T(8,128)(2,1)S(1)} %pad_maximum_fusion.6), channel_id=1, source_target_pairs={{0,4},{1,5},{2,6},{3,7},{4,0},{5,1},{6,2},{7,3},{8,12},{9,13},{10,... | collective-permute-start | bytes 221192 | tf_op jit(solution)/shard_map/ppermute | solution.py:44
  18.5 7.4 %collective-permute-start.18 = (bf16[3,54,576]{2,1,0:T(8,128)(2,1)S(1)}, bf16[3,54,576]{2,1,0:T(8,128)(2,1)S(1)}, u32[]{:S(2)}, u32[]{:S(2)}) collective-permute-start(bf16[3,54,576]{2,1,0:T(8,128)(2,1)S(1)} %fusion.21), channel_id=1, source_target_pairs={{0,4},{1,5},{2,6},{3,7},{4,0},{5,1},{6,2},{7,3},{8,12},{9,13},{10,... | collective-permute-start | bytes 559880 | tf_op jit(solution)/shard_map/ppermute | solution.py:44
  27.7 44.3 %all-to-all-start = ((bf16[16,72,1024]{2,1,0:T(8,128)(2,1)}), bf16[16,72,1024]{2,1,0:T(8,128)(2,1)S(1)}, u32[]{:S(2)}, u32[]{:S(2)}) async-start(bf16[16,72,1024]{2,1,0:T(8,128)(2,1)} %broadcast_in_dim.40), calls=%async_computation | async-start | bytes 4718592 | tf_op jit(solution)/shard_map/all_to_all | solution.py:79
  35.7 252.8 %reduce-scatter.2.cloned.1.call-start = ((), (), s32[]{:S(2)}) async-start(), calls=%async_computation.7 | async-start | bytes 7520256 | tf_op jit(solution)/shard_map/reduce_scatter | solution.py:616
  39.7 16.5 %collective-permute-start.5 = (bf16[128,1152]{1,0:T(8,128)(2,1)S(1)}, bf16[128,1152]{1,0:T(8,128)(2,1)}, u32[]{:S(2)}, u32[]{:S(2)}) collective-permute-start(bf16[128,1152]{1,0:T(8,128)(2,1)S(1)} %fusion.12.refs_0_.refs_4_), channel_id=1, source_target_pairs={{0,6},{1,7},{2,4},{3,5},{4,2},{5,3},{6,0},{7,1},{8,14},{9,15},{10,... | collective-permute-start | bytes 884744 | tf_op jit(solution)/shard_map/ppermute | solution.py:44
  42.1 15.0 %collective-permute-start.4 = (bf16[128,1152]{1,0:T(8,128)(2,1)S(1)}, bf16[128,1152]{1,0:T(8,128)(2,1)}, u32[]{:S(2)}, u32[]{:S(2)}) collective-permute-start(bf16[128,1152]{1,0:T(8,128)(2,1)S(1)} %fusion.12.refs_0_.refs_4_), channel_id=1, source_target_pairs={{0,4},{1,5},{2,6},{3,7},{4,0},{5,1},{6,2},{7,3},{8,12},{9,13},{10,... | collective-permute-start | bytes 884744 | tf_op jit(solution)/shard_map/ppermute | solution.py:44
  42.2 15.0 %collective-permute-start.1 = (bf16[128,1152]{1,0:T(8,128)(2,1)S(1)}, bf16[128,1152]{1,0:T(8,128)(2,1)}, u32[]{:S(2)}, u32[]{:S(2)}) collective-permute-start(bf16[128,1152]{1,0:T(8,128)(2,1)S(1)} %fusion.12.refs_0_.refs_4_), channel_id=1, source_target_pairs={{0,2},{1,3},{2,0},{3,1},{4,6},{5,7},{6,4},{7,5},{8,10},{9,11},{10,... | collective-permute-start | bytes 884744 | tf_op jit(solution)/shard_map/ppermute | solution.py:44
  45.3 26.8 %collective-permute-start.2 = (bf16[128,1152]{1,0:T(8,128)(2,1)S(1)}, bf16[128,1152]{1,0:T(8,128)(2,1)}, u32[]{:S(2)}, u32[]{:S(2)}) collective-permute-start(bf16[128,1152]{1,0:T(8,128)(2,1)S(1)} %fusion.12.refs_0_.refs_4_), channel_id=1, source_target_pairs={{0,1},{1,0},{2,3},{3,2},{4,5},{5,4},{6,7},{7,6},{8,9},{9,8},{10,11... | collective-permute-start | bytes 884744 | tf_op jit(solution)/shard_map/ppermute | solution.py:44
  56.2 15.8 %collective-permute-start.7 = (bf16[128,1152]{1,0:T(8,128)(2,1)}, bf16[128,1152]{1,0:T(8,128)(2,1)}, u32[]{:S(2)}, u32[]{:S(2)}) collective-permute-start(bf16[128,1152]{1,0:T(8,128)(2,1)} %collective-permute-done.5.refs_5_.refs_9_), channel_id=1, source_target_pairs={{0,1},{1,0},{2,3},{3,2},{4,5},{5,4},{6,7},{7,6},{8,9},{9,8},{10,11... | collective-permute-start | bytes 884744 | tf_op jit(solution)/shard_map/ppermute | solution.py:44
  57.2 14.9 %collective-permute-start.6 = (bf16[128,1152]{1,0:T(8,128)(2,1)}, bf16[128,1152]{1,0:T(8,128)(2,1)}, u32[]{:S(2)}, u32[]{:S(2)}) collective-permute-start(bf16[128,1152]{1,0:T(8,128)(2,1)} %collective-permute-done.4.refs_4_.refs_8_), channel_id=1, source_target_pairs={{0,1},{1,0},{2,3},{3,2},{4,5},{5,4},{6,7},{7,6},{8,9},{9,8},{10,11... | collective-permute-start | bytes 884744 | tf_op jit(solution)/shard_map/ppermute | solution.py:44
  57.3 14.8 %collective-permute-start.3 = (bf16[128,1152]{1,0:T(8,128)(2,1)}, bf16[128,1152]{1,0:T(8,128)(2,1)}, u32[]{:S(2)}, u32[]{:S(2)}) collective-permute-start(bf16[128,1152]{1,0:T(8,128)(2,1)} %collective-permute-done.1.refs_1_.refs_5_), channel_id=1, source_target_pairs={{0,1},{1,0},{2,3},{3,2},{4,5},{5,4},{6,7},{7,6},{8,9},{9,8},{10,11... | collective-permute-start | bytes 884744 | tf_op jit(solution)/shard_map/ppermute | solution.py:44
  79.7 5.6 %collective-permute-start.9 = (bf16[128,1152]{1,0:T(8,128)(2,1)S(1)}, bf16[128,1152]{1,0:T(8,128)(2,1)S(1)}, u32[]{:S(2)}, u32[]{:S(2)}) collective-permute-start(bf16[128,1152]{1,0:T(8,128)(2,1)S(1)} %get-tuple-element.105), channel_id=1, source_target_pairs={{0,1},{1,0},{2,3},{3,2},{4,5},{5,4},{6,7},{7,6},{8,9},{9,8},{10,11... | collective-permute-start | bytes 884744 | tf_op jit(solution)/shard_map/ppermute | solution.py:44
  85.4 8.4 %collective-permute-start.10 = (bf16[128,1152]{1,0:T(8,128)(2,1)S(1)}, bf16[128,1152]{1,0:T(8,128)(2,1)S(1)}, u32[]{:S(2)}, u32[]{:S(2)}) collective-permute-start(bf16[128,1152]{1,0:T(8,128)(2,1)S(1)} %add_convert_fusion.10), channel_id=1, source_target_pairs={{0,2},{1,3},{2,0},{3,1},{4,6},{5,7},{6,4},{7,5},{8,10},{9,11},{10,... | collective-permute-start | bytes 884744 | tf_op jit(solution)/shard_map/ppermute | solution.py:44
  95.8 16.6 %collective-permute-start.15 = (bf16[128,1152]{1,0:T(8,128)(2,1)S(1)}, bf16[128,1152]{1,0:T(8,128)(2,1)S(1)}, u32[]{:S(2)}, u32[]{:S(2)}) collective-permute-start(bf16[128,1152]{1,0:T(8,128)(2,1)S(1)} %multiply_convert_fusion.refs_0_), channel_id=1, source_target_pairs={{0,6},{1,7},{2,4},{3,5},{4,2},{5,3},{6,0},{7,1},{8,14},{9,15},{10,... | collective-permute-start | bytes 884744 | tf_op jit(solution)/shard_map/ppermute | solution.py:44
  99.7 14.3 %collective-permute-start.14 = (bf16[128,1152]{1,0:T(8,128)(2,1)S(1)}, bf16[128,1152]{1,0:T(8,128)(2,1)S(1)}, u32[]{:S(2)}, u32[]{:S(2)}) collective-permute-start(bf16[128,1152]{1,0:T(8,128)(2,1)S(1)} %multiply_convert_fusion.refs_0_), channel_id=1, source_target_pairs={{0,4},{1,5},{2,6},{3,7},{4,0},{5,1},{6,2},{7,3},{8,12},{9,13},{10,... | collective-permute-start | bytes 884744 | tf_op jit(solution)/shard_map/ppermute | solution.py:44
  99.9 14.2 %collective-permute-start.11 = (bf16[128,1152]{1,0:T(8,128)(2,1)S(1)}, bf16[128,1152]{1,0:T(8,128)(2,1)S(1)}, u32[]{:S(2)}, u32[]{:S(2)}) collective-permute-start(bf16[128,1152]{1,0:T(8,128)(2,1)S(1)} %multiply_convert_fusion.refs_0_), channel_id=1, source_target_pairs={{0,2},{1,3},{2,0},{3,1},{4,6},{5,7},{6,4},{7,5},{8,10},{9,11},{10,... | collective-permute-start | bytes 884744 | tf_op jit(solution)/shard_map/ppermute | solution.py:44
  100.4 14.3 %collective-permute-start.12 = (bf16[128,1152]{1,0:T(8,128)(2,1)S(1)}, bf16[128,1152]{1,0:T(8,128)(2,1)S(1)}, u32[]{:S(2)}, u32[]{:S(2)}) collective-permute-start(bf16[128,1152]{1,0:T(8,128)(2,1)S(1)} %multiply_convert_fusion.refs_0_), channel_id=1, source_target_pairs={{0,1},{1,0},{2,3},{3,2},{4,5},{5,4},{6,7},{7,6},{8,9},{9,8},{10,11... | collective-permute-start | bytes 884744 | tf_op jit(solution)/shard_map/ppermute | solution.py:44
  129.6 5.1 %collective-permute-start.19 = (bf16[128,1152]{1,0:T(8,128)(2,1)S(1)}, bf16[128,1152]{1,0:T(8,128)(2,1)S(1)}, u32[]{:S(2)}, u32[]{:S(2)}) collective-permute-start(bf16[128,1152]{1,0:T(8,128)(2,1)S(1)} %get-tuple-element.109), channel_id=1, source_target_pairs={{0,1},{1,0},{2,3},{3,2},{4,5},{5,4},{6,7},{7,6},{8,9},{9,8},{10,11... | collective-permute-start | bytes 884744 | tf_op jit(solution)/shard_map/ppermute | solution.py:44
  131.0 9.9 %collective-permute-start.21 = (bf16[128,1152]{1,0:T(8,128)(2,1)S(1)}, bf16[128,1152]{1,0:T(8,128)(2,1)S(1)}, u32[]{:S(2)}, u32[]{:S(2)}) collective-permute-start(bf16[128,1152]{1,0:T(8,128)(2,1)S(1)} %add_convert_fusion.9), channel_id=1, source_target_pairs={{0,4},{1,5},{2,6},{3,7},{4,0},{5,1},{6,2},{7,3},{8,12},{9,13},{10,... | collective-permute-start | bytes 884744 | tf_op jit(solution)/shard_map/ppermute | solution.py:44
  133.7 14.2 %collective-permute-start.23 = (bf16[128,1152]{1,0:T(8,128)(2,1)S(1)}, bf16[128,1152]{1,0:T(8,128)(2,1)S(1)}, u32[]{:S(2)}, u32[]{:S(2)}) collective-permute-start(bf16[128,1152]{1,0:T(8,128)(2,1)S(1)} %add_convert_fusion.8), channel_id=1, source_target_pairs={{0,6},{1,7},{2,4},{3,5},{4,2},{5,3},{6,0},{7,1},{8,14},{9,15},{10,... | collective-permute-start | bytes 884744 | tf_op jit(solution)/shard_map/ppermute | solution.py:44
  134.7 13.2 %collective-permute-start.25 = (bf16[128,1152]{1,0:T(8,128)(2,1)S(1)}, bf16[128,1152]{1,0:T(8,128)(2,1)S(1)}, u32[]{:S(2)}, u32[]{:S(2)}) collective-permute-start(bf16[128,1152]{1,0:T(8,128)(2,1)S(1)} %add_convert_fusion.7), channel_id=1, source_target_pairs={{0,2},{1,3},{2,0},{3,1},{4,6},{5,7},{6,4},{7,5},{8,10},{9,11},{10,... | collective-permute-start | bytes 884744 | tf_op jit(solution)/shard_map/ppermute | solution.py:44
  149.9 15.4 %collective-permute-start.30 = (bf16[128,1152]{1,0:T(8,128)(2,1)S(1)}, bf16[128,1152]{1,0:T(8,128)(2,1)S(1)}, u32[]{:S(2)}, u32[]{:S(2)}) collective-permute-start(bf16[128,1152]{1,0:T(8,128)(2,1)S(1)} %get-tuple-element.263.refs_8_), channel_id=1, source_target_pairs={{0,6},{1,7},{2,4},{3,5},{4,2},{5,3},{6,0},{7,1},{8,14},{9,15},{10,... | collective-permute-start | bytes 884744 | tf_op jit(solution)/shard_map/ppermute | solution.py:44
  152.6 14.3 %collective-permute-start.29 = (bf16[128,1152]{1,0:T(8,128)(2,1)S(1)}, bf16[128,1152]{1,0:T(8,128)(2,1)S(1)}, u32[]{:S(2)}, u32[]{:S(2)}) collective-permute-start(bf16[128,1152]{1,0:T(8,128)(2,1)S(1)} %get-tuple-element.263.refs_8_), channel_id=1, source_target_pairs={{0,4},{1,5},{2,6},{3,7},{4,0},{5,1},{6,2},{7,3},{8,12},{9,13},{10,... | collective-permute-start | bytes 884744 | tf_op jit(solution)/shard_map/ppermute | solution.py:44
  152.6 14.3 %collective-permute-start.26 = (bf16[128,1152]{1,0:T(8,128)(2,1)S(1)}, bf16[128,1152]{1,0:T(8,128)(2,1)S(1)}, u32[]{:S(2)}, u32[]{:S(2)}) collective-permute-start(bf16[128,1152]{1,0:T(8,128)(2,1)S(1)} %get-tuple-element.263.refs_8_), channel_id=1, source_target_pairs={{0,2},{1,3},{2,0},{3,1},{4,6},{5,7},{6,4},{7,5},{8,10},{9,11},{10,... | collective-permute-start | bytes 884744 | tf_op jit(solution)/shard_map/ppermute | solution.py:44
  153.2 22.9 %collective-permute-start.27 = (bf16[128,1152]{1,0:T(8,128)(2,1)S(1)}, bf16[128,1152]{1,0:T(8,128)(2,1)S(1)}, u32[]{:S(2)}, u32[]{:S(2)}) collective-permute-start(bf16[128,1152]{1,0:T(8,128)(2,1)S(1)} %get-tuple-element.263.refs_8_), channel_id=1, source_target_pairs={{0,1},{1,0},{2,3},{3,2},{4,5},{5,4},{6,7},{7,6},{8,9},{9,8},{10,11... | collective-permute-start | bytes 884744 | tf_op jit(solution)/shard_map/ppermute | solution.py:44
  165.3 10.7 %collective-permute-start.32 = (bf16[128,1152]{1,0:T(8,128)(2,1)S(1)}, bf16[128,1152]{1,0:T(8,128)(2,1)S(1)}, u32[]{:S(2)}, u32[]{:S(2)}) collective-permute-start(bf16[128,1152]{1,0:T(8,128)(2,1)S(1)} %collective-permute-done.30.refs_13_), channel_id=1, source_target_pairs={{0,1},{1,0},{2,3},{3,2},{4,5},{5,4},{6,7},{7,6},{8,9},{9,8},{10,11... | collective-permute-start | bytes 884744 | tf_op jit(solution)/shard_map/ppermute | solution.py:44
  166.9 9.2 %collective-permute-start.31 = (bf16[128,1152]{1,0:T(8,128)(2,1)S(1)}, bf16[128,1152]{1,0:T(8,128)(2,1)S(1)}, u32[]{:S(2)}, u32[]{:S(2)}) collective-permute-start(bf16[128,1152]{1,0:T(8,128)(2,1)S(1)} %collective-permute-done.29.refs_12_), channel_id=1, source_target_pairs={{0,1},{1,0},{2,3},{3,2},{4,5},{5,4},{6,7},{7,6},{8,9},{9,8},{10,11... | collective-permute-start | bytes 884744 | tf_op jit(solution)/shard_map/ppermute | solution.py:44
  166.9 10.5 %collective-permute-start.28 = (bf16[128,1152]{1,0:T(8,128)(2,1)S(1)}, bf16[128,1152]{1,0:T(8,128)(2,1)S(1)}, u32[]{:S(2)}, u32[]{:S(2)}) collective-permute-start(bf16[128,1152]{1,0:T(8,128)(2,1)S(1)} %collective-permute-done.26.refs_9_), channel_id=1, source_target_pairs={{0,1},{1,0},{2,3},{3,2},{4,5},{5,4},{6,7},{7,6},{8,9},{9,8},{10,11... | collective-permute-start | bytes 884744 | tf_op jit(solution)/shard_map/ppermute | solution.py:44
  202.2 5.2 %collective-permute-start.33 = (bf16[128,1152]{1,0:T(8,128)(2,1)S(1)}, bf16[128,1152]{1,0:T(8,128)(2,1)S(1)}, u32[]{:S(2)}, u32[]{:S(2)}) collective-permute-start(bf16[128,1152]{1,0:T(8,128)(2,1)S(1)} %get-tuple-element.122), channel_id=1, source_target_pairs={{0,1},{1,0},{2,3},{3,2},{4,5},{5,4},{6,7},{7,6},{8,9},{9,8},{10,11... | collective-permute-start | bytes 884744 | tf_op jit(solution)/shard_map/ppermute | solution.py:44
  203.6 10.0 %collective-permute-start.35 = (bf16[128,1152]{1,0:T(8,128)(2,1)S(1)}, bf16[128,1152]{1,0:T(8,128)(2,1)S(1)}, u32[]{:S(2)}, u32[]{:S(2)}) collective-permute-start(bf16[128,1152]{1,0:T(8,128)(2,1)S(1)} %add_convert_fusion.5), channel_id=1, source_target_pairs={{0,4},{1,5},{2,6},{3,7},{4,0},{5,1},{6,2},{7,3},{8,12},{9,13},{10,... | collective-permute-start | bytes 884744 | tf_op jit(solution)/shard_map/ppermute | solution.py:44
  205.7 14.8 %collective-permute-start.37 = (bf16[128,1152]{1,0:T(8,128)(2,1)S(1)}, bf16[128,1152]{1,0:T(8,128)(2,1)S(1)}, u32[]{:S(2)}, u32[]{:S(2)}) collective-permute-start(bf16[128,1152]{1,0:T(8,128)(2,1)S(1)} %add_convert_fusion.4), channel_id=1, source_target_pairs={{0,6},{1,7},{2,4},{3,5},{4,2},{5,3},{6,0},{7,1},{8,14},{9,15},{10,... | collective-permute-start | bytes 884744 | tf_op jit(solution)/shard_map/ppermute | solution.py:44
  207.3 13.2 %collective-permute-start.39 = (bf16[128,1152]{1,0:T(8,128)(2,1)S(1)}, bf16[128,1152]{1,0:T(8,128)(2,1)S(1)}, u32[]{:S(2)}, u32[]{:S(2)}) collective-permute-start(bf16[128,1152]{1,0:T(8,128)(2,1)S(1)} %add_convert_fusion.3), channel_id=1, source_target_pairs={{0,2},{1,3},{2,0},{3,1},{4,6},{5,7},{6,4},{7,5},{8,10},{9,11},{10,... | collective-permute-start | bytes 884744 | tf_op jit(solution)/shard_map/ppermute | solution.py:44
  222.9 8.1 %collective-permute-start.40 = (bf16[128,1152]{1,0:T(8,128)(2,1)S(1)}, bf16[128,1152]{1,0:T(8,128)(2,1)S(1)}, u32[]{:S(2)}, u32[]{:S(2)}) collective-permute-start(bf16[128,1152]{1,0:T(8,128)(2,1)S(1)} %subtract_convert_fusion.refs_0_), channel_id=1, source_target_pairs={{0,2},{1,3},{2,0},{3,1},{4,6},{5,7},{6,4},{7,5},{8,10},{9,11},{10,... | collective-permute-start | bytes 884744 | tf_op jit(solution)/shard_map/ppermute | solution.py:44
  224.0 8.6 %collective-permute-start.41 = (bf16[128,1152]{1,0:T(8,128)(2,1)S(1)}, bf16[128,1152]{1,0:T(8,128)(2,1)S(1)}, u32[]{:S(2)}, u32[]{:S(2)}) collective-permute-start(bf16[128,1152]{1,0:T(8,128)(2,1)S(1)} %subtract_convert_fusion.refs_0_), channel_id=1, source_target_pairs={{0,1},{1,0},{2,3},{3,2},{4,5},{5,4},{6,7},{7,6},{8,9},{9,8},{10,11... | collective-permute-start | bytes 884744 | tf_op jit(solution)/shard_map/ppermute | solution.py:44
  243.6 5.6 %collective-permute-start.44 = (bf16[128,1152]{1,0:T(8,128)(2,1)S(1)}, bf16[128,1152]{1,0:T(8,128)(2,1)}, u32[]{:S(2)}, u32[]{:S(2)}) collective-permute-start(bf16[128,1152]{1,0:T(8,128)(2,1)S(1)} %get-tuple-element.140), channel_id=1, source_target_pairs={{0,1},{1,0},{2,3},{3,2},{4,5},{5,4},{6,7},{7,6},{8,9},{9,8},{10,11... | collective-permute-start | bytes 884744 | tf_op jit(solution)/shard_map/ppermute | solution.py:44
  244.0 48.5 %all-to-all-start.1 = ((bf16[16,72,1024]{2,1,0:T(8,128)(2,1)}), bf16[16,72,1024]{2,1,0:T(8,128)(2,1)}, u32[]{:S(2)}, u32[]{:S(2)}) async-start(bf16[16,72,1024]{2,1,0:T(8,128)(2,1)} %get-tuple-element.146), calls=%async_computation.1 | async-start | bytes 4718592 | tf_op jit(solution)/shard_map/all_to_all | solution.py:79
  248.5 5.5 %collective-permute-start.43 = (bf16[128,1152]{1,0:T(8,128)(2,1)S(1)}, bf16[128,1152]{1,0:T(8,128)(2,1)S(1)}, u32[]{:S(2)}, u32[]{:S(2)}) collective-permute-start(bf16[128,1152]{1,0:T(8,128)(2,1)S(1)} %get-tuple-element.138), channel_id=1, source_target_pairs={{0,1},{1,0},{2,3},{3,2},{4,5},{5,4},{6,7},{7,6},{8,9},{9,8},{10,11... | collective-permute-start | bytes 884744 | tf_op jit(solution)/shard_map/ppermute | solution.py:44
  249.1 4.6 %collective-permute-start.48 = (bf16[128,1152]{1,0:T(8,128)(2,1)S(1)}, bf16[128,1152]{1,0:T(8,128)(2,1)S(1)}, u32[]{:S(2)}, u32[]{:S(2)}) collective-permute-start(bf16[128,1152]{1,0:T(8,128)(2,1)S(1)} %get-tuple-element.144), channel_id=1, source_target_pairs={{0,1},{1,0},{2,3},{3,2},{4,5},{5,4},{6,7},{7,6},{8,9},{9,8},{10,11... | collective-permute-start | bytes 884744 | tf_op jit(solution)/shard_map/ppermute | solution.py:44
  250.3 9.9 %collective-permute-start.45 = (bf16[128,1152]{1,0:T(8,128)(2,1)S(1)}, bf16[128,1152]{1,0:T(8,128)(2,1)S(1)}, u32[]{:S(2)}, u32[]{:S(2)}) collective-permute-start(bf16[128,1152]{1,0:T(8,128)(2,1)S(1)} %add_convert_fusion.2), channel_id=1, source_target_pairs={{0,4},{1,5},{2,6},{3,7},{4,0},{5,1},{6,2},{7,3},{8,12},{9,13},{10,... | collective-permute-start | bytes 884744 | tf_op jit(solution)/shard_map/ppermute | solution.py:44
  252.8 14.4 %collective-permute-start.47 = (bf16[128,1152]{1,0:T(8,128)(2,1)S(1)}, bf16[128,1152]{1,0:T(8,128)(2,1)S(1)}, u32[]{:S(2)}, u32[]{:S(2)}) collective-permute-start(bf16[128,1152]{1,0:T(8,128)(2,1)S(1)} %add_convert_fusion.1), channel_id=1, source_target_pairs={{0,6},{1,7},{2,4},{3,5},{4,2},{5,3},{6,0},{7,1},{8,14},{9,15},{10,... | collective-permute-start | bytes 884744 | tf_op jit(solution)/shard_map/ppermute | solution.py:44
  253.8 13.4 %collective-permute-start.49 = (bf16[128,1152]{1,0:T(8,128)(2,1)S(1)}, bf16[128,1152]{1,0:T(8,128)(2,1)S(1)}, u32[]{:S(2)}, u32[]{:S(2)}) collective-permute-start(bf16[128,1152]{1,0:T(8,128)(2,1)S(1)} %add_convert_fusion), channel_id=1, source_target_pairs={{0,2},{1,3},{2,0},{3,1},{4,6},{5,7},{6,4},{7,5},{8,10},{9,11},{10,... | collective-permute-start | bytes 884744 | tf_op jit(solution)/shard_map/ppermute | solution.py:44
  289.7 8.5 %collective-permute-start.53 = (bf16[192,576]{1,0:T(8,128)(2,1)S(1)}, bf16[192,576]{1,0:T(8,128)(2,1)S(1)}, u32[]{:S(2)}, u32[]{:S(2)}) collective-permute-start(bf16[192,576]{1,0:T(8,128)(2,1)S(1)} %get-tuple-element.266), channel_id=1, source_target_pairs={{0,4},{1,5},{2,6},{3,7},{4,0},{5,1},{6,2},{7,3},{8,12},{9,13},{10,... | collective-permute-start | bytes 663560 | tf_op jit(solution)/shard_map/ppermute | solution.py:44
  303.2 33.5 %all-to-all-start.2 = ((f32[16,240,128]{2,1,0:T(8,128)}), f32[16,240,128]{2,1,0:T(8,128)}, u32[]{:S(2)}, u32[]{:S(2)}) async-start(f32[16,240,128]{2,1,0:T(8,128)} %get-tuple-element.152), calls=%async_computation.3 | async-start | bytes 3932160 | tf_op jit(solution)/shard_map/all_to_all | solution.py:79
  310.1 6.4 %collective-permute-start.50 = (f32[41,1024]{1,0:T(8,128)S(1)}, f32[41,1024]{1,0:T(8,128)S(1)}, u32[]{:S(2)}, u32[]{:S(2)}) collective-permute-start(f32[41,1024]{1,0:T(8,128)S(1)} %pad_maximum_fusion.1), channel_id=1, source_target_pairs={{0,4},{1,5},{2,6},{3,7},{4,0},{5,1},{6,2},{7,3},{8,12},{9,13},{10,... | collective-permute-start | bytes 503816 | tf_op jit(solution)/shard_map/ppermute | solution.py:44
  339.5 20.3 %all-to-all-start.4 = ((f32[16,120,128]{2,1,0:T(8,128)}), f32[16,120,128]{2,1,0:T(8,128)S(1)}, u32[]{:S(2)}, u32[]{:S(2)}) async-start(f32[16,120,128]{2,1,0:T(8,128)} %broadcast_in_dim.52), calls=%async_computation.5 | async-start | bytes 1966080 | tf_op jit(solution)/shard_map/all_to_all | solution.py:79
  345.1 63.4 %all-gather.5.cloned.1.call-start = ((), (), s32[]{:S(2)}) async-start(), calls=%async_computation.8 | async-start | bytes 3203072 | tf_op jit(solution)/shard_map/all_gather | solution.py:717
  360.9 27.2 %all-to-all-start.3 = ((f32[16,120,128]{2,1,0:T(8,128)}), f32[16,120,128]{2,1,0:T(8,128)S(1)}, u32[]{:S(2)}, u32[]{:S(2)}) async-start(f32[16,120,128]{2,1,0:T(8,128)} %broadcast_in_dim.51), calls=%async_computation.4 | async-start | bytes 1966080 | tf_op jit(solution)/shard_map/all_to_all | solution.py:79
  (80 other events, 956.3 us)
Sparse Core Ops, SparseCore 0:
  27.0 86.3 all-gather.2
  193.1 95.3 reduce-scatter.1
  348.2 57.8 all-gather.4
